TPU v7x, 256 devices: a whole 4x4x8 slice. The times are simulated.
256 devices in a mesh: lat: 8 (over y, x_hi), lon: 32 (over z, x_lo, core).
Axes of the slice: x: 4 (x_hi: 2, x_lo: 2; x = x_hi * 2 + x_lo), y: 4, z: 8, core: 2. Of those that a mesh axis runs over, the one named last changes fastest.
Arguments:
- tokens: bfloat16 [2, 48, 384, 192], P(None, 'lat', 'lon'), may hold values from -6 to 6
- grad_mixed: bfloat16 [2, 48, 384, 192], P(None, 'lat', 'lon'), may hold values from -6 to 6
- w_qkv: bfloat16 [2, 192, 576], replicated, may hold values from -0.4375 to 0.4375
- w_proj: bfloat16 [2, 192, 192], replicated, may hold values from -0.4375 to 0.4375
- w_up: bfloat16 [2, 192, 768], replicated, may hold values from -0.4375 to 0.4375
- w_down: bfloat16 [2, 768, 192], replicated, may hold values from -0.21875 to 0.21875
- gains: float32 [2, 2, 192], replicated, may hold values from 0.5 to 1.5
- bias_table: float32 [2, 1, 8, 6, 3312], P(None, None, 'lat'), may hold values from -300 to 300
- rel_index: int32 [144, 144], replicated, may hold values from 0 to 3311
- mask_ids: int32 [48], P('lat'), may hold values from 0 to 15, never falling along the last dimension, each value on 1 to 6 neighbouring positions
Outputs:
- mixed: bfloat16 [2, 48, 384, 192], P(None, 'lat', 'lon')
- grad_tokens: bfloat16 [2, 48, 384, 192], P(None, 'lat', 'lon')
- grad_qkv: float32 [2, 192, 576], P(None, None, 'lon')
- grad_proj: float32 [2, 192, 192], P(None, None, 'lon')
- grad_up: float32 [2, 192, 768], P(None, None, 'lon')
- grad_down: float32 [2, 768, 192], P(None, None, 'lon')
- grad_table: float32 [2, 1, 8, 6, 3312], P(None, None, 'lat')
Inputs may be any that keep to these rules, and one draw needn't show every extreme that they name: `mask_ids`: ids never fall along the rows; a run of one id covers at most 6 rows.
All inputs are finite; a program needn't handle non-finite values.
Results may differ from a plain program's by a relative error of at most 0.04.
Values may be sent and summed in bfloat16 or wider, within the bound.
A program may use at most 64 MiB of HBM per device.

v0:
```python
import jax
import jax.numpy as jnp
from jax import lax
from jax.sharding import PartitionSpec as P

HEADS = 6


EPS = 1e-05
NEGATIVE = -1e30


def passed_along(value, axis, steps):
    count = lax.axis_size(axis)
    pairs = [(source, (source + steps) % count) for source in range(count)]
    return lax.ppermute(value, axis, pairs)


def to_windows(field):
    levels, n_rows, n_cols, n_feat = field.shape
    blocks = field.reshape(levels // 2, 2, n_rows // 6, 6, n_cols // 12, 12, n_feat)
    blocks = blocks.transpose(0, 2, 4, 1, 3, 5, 6)
    return blocks.reshape(levels // 2, n_rows // 6, n_cols // 12, 144, n_feat)


def from_windows(windows):
    lev_win, lat_win, lon_win, tok_win, n_feat = windows.shape
    blocks = windows.reshape(lev_win, lat_win, lon_win, 2, 6, 12, n_feat)
    blocks = blocks.transpose(0, 3, 1, 4, 2, 5, 6)
    return blocks.reshape(lev_win * 2, lat_win * 6, lon_win * 12, n_feat)


def window_mask(levels, lat_ids, shifted):
    places = jnp.arange(144, dtype=jnp.int32)
    level_off = places // 72
    row_off = places // 12 % 6
    level_of = 2 * jnp.arange(levels // 2, dtype=jnp.int32)[:, None] + level_off[None, :]
    region = jnp.where(level_of < levels - 2, 0, jnp.where(level_of < levels - 1, 1, 2))
    row_ids = lat_ids.reshape(-1, 6)[:, row_off]
    same_level = region[:, :, None] == region[:, None, :]
    same_row = row_ids[:, :, None] == row_ids[:, None, :]
    allowed = same_level[:, None] & same_row[None]
    if not shifted:
        allowed = jnp.ones_like(allowed)
    return allowed


def norm_rows(inner, gain):
    center = inner - jnp.mean(inner, axis=-1, keepdims=True)
    spread = jnp.mean(center * center, axis=-1, keepdims=True)
    return center * lax.rsqrt(spread + EPS) * gain


def matmul(left, right):
    return jnp.dot(left, right, preferred_element_type=jnp.float32)


def mat_tn(left, right):
    return lax.dot_general(
        left, right, (((0,), (0,)), ((), ())), preferred_element_type=jnp.float32
    )


def mat_nt(left, right):
    return lax.dot_general(
        left, right, (((1,), (1,)), ((), ())), preferred_element_type=jnp.float32
    )


def attend(qkv, bias, allowed):
    lev_win, lat_win, lon_win, n_tok, triple = qkv.shape
    n_feat = triple // 3
    unpacked = qkv.astype(jnp.float32).reshape(
        lev_win, lat_win, lon_win, n_tok, 3, HEADS, n_feat // HEADS
    )
    q_heads = unpacked[:, :, :, :, 0]
    k_heads = unpacked[:, :, :, :, 1]
    v_heads = unpacked[:, :, :, :, 2]
    scaling = (n_feat // HEADS) ** (-0.5)
    score_mat = jnp.einsum("abcshe,abcthe->abchst", q_heads, k_heads) * scaling + bias[:, :, None]
    score_mat = jnp.where(allowed[:, :, None, None], score_mat, NEGATIVE)
    row_max = jnp.max(score_mat, axis=-1, keepdims=True)
    exp_scores = jnp.exp(score_mat - row_max)
    att_probs = exp_scores / jnp.sum(exp_scores, axis=-1, keepdims=True)
    att_weights = att_probs.astype(jnp.bfloat16)
    attended = jnp.einsum("abchst,abcthe->abcshe", att_weights.astype(jnp.float32), v_heads)
    attended = attended.reshape(lev_win, lat_win, lon_win, n_tok, n_feat).astype(jnp.bfloat16)
    return (attended, (att_probs, att_weights, q_heads, k_heads, v_heads))


def attend_back(grad_att, att_saved):
    att_probs, att_weights, q_heads, k_heads, v_heads = att_saved
    lev_win, lat_win, lon_win, n_tok, n_feat = grad_att.shape
    grad_heads = grad_att.astype(jnp.float32).reshape(
        lev_win, lat_win, lon_win, n_tok, HEADS, n_feat // HEADS
    )
    scaling = (n_feat // HEADS) ** (-0.5)
    grad_probs = jnp.einsum("abcshe,abcthe->abchst", grad_heads, v_heads)
    grad_v = jnp.einsum("abchst,abcshe->abcthe", att_weights.astype(jnp.float32), grad_heads)
    grad_scores = att_probs * (grad_probs - jnp.sum(grad_probs * att_probs, axis=-1, keepdims=True))
    grad_q = jnp.einsum("abchst,abcthe->abcshe", grad_scores, k_heads) * scaling
    grad_k = jnp.einsum("abchst,abcshe->abcthe", grad_scores, q_heads) * scaling
    grad_qkv = jnp.stack([grad_q, grad_k, grad_v], axis=4)
    grad_qkv = grad_qkv.reshape(lev_win, lat_win, lon_win, n_tok, 3 * n_feat).astype(jnp.bfloat16)
    return (grad_qkv, jnp.sum(grad_scores, axis=2))


def block_forward(windows, weights, bias, allowed):
    w_qkv, w_proj, w_up, w_down, gains = weights
    win_shape = windows.shape
    n_feat = win_shape[-1]
    flat_in = windows.reshape(-1, n_feat)
    qkv = matmul(flat_in, w_qkv).astype(jnp.bfloat16).reshape(win_shape[:-1] + (3 * n_feat,))
    attended, att_saved = attend(qkv, bias, allowed)
    flat_att = attended.reshape(-1, n_feat)
    pre_norm = matmul(flat_att, w_proj)
    middle = (flat_in.astype(jnp.float32) + norm_rows(pre_norm, gains[0])).astype(jnp.bfloat16)
    up_out = matmul(middle, w_up)
    hidden = jax.nn.gelu(up_out, approximate=False).astype(jnp.bfloat16)
    down_out = matmul(hidden, w_down)
    result = (middle.astype(jnp.float32) + norm_rows(down_out, gains[1])).astype(jnp.bfloat16)
    saved = (flat_in, flat_att, pre_norm, middle, up_out, hidden, down_out, att_saved)
    return (result.reshape(win_shape), saved)


def block_backward(grad_res, saved, weights):
    w_qkv, w_proj, w_up, w_down, gains = weights
    flat_in, flat_att, pre_norm, middle, up_out, hidden, down_out, att_saved = saved
    win_shape = grad_res.shape
    n_feat = win_shape[-1]
    grad_out = grad_res.reshape(-1, n_feat).astype(jnp.float32)
    pullback = jax.vjp(lambda inner: norm_rows(inner, gains[1]), down_out)[1]
    grad_down_out = pullback(grad_out)[0].astype(jnp.bfloat16)
    d_down = mat_tn(hidden, grad_down_out)
    grad_hidden = mat_nt(grad_down_out, w_down)
    pullback = jax.vjp(lambda inner: jax.nn.gelu(inner, approximate=False), up_out)[1]
    grad_up_out = pullback(grad_hidden)[0].astype(jnp.bfloat16)
    d_up = mat_tn(middle, grad_up_out)
    grad_middle = grad_out + mat_nt(grad_up_out, w_up)
    pullback = jax.vjp(lambda inner: norm_rows(inner, gains[0]), pre_norm)[1]
    grad_pre = pullback(grad_middle)[0].astype(jnp.bfloat16)
    d_proj = mat_tn(flat_att, grad_pre)
    grad_att = mat_nt(grad_pre, w_proj).astype(jnp.bfloat16).reshape(win_shape)
    grad_qkv, grad_bias = attend_back(grad_att, att_saved)
    flat_grad = grad_qkv.reshape(-1, 3 * n_feat)
    d_qkv = mat_tn(flat_in, flat_grad)
    grad_in = (grad_middle + mat_nt(flat_grad, w_qkv)).astype(jnp.bfloat16).reshape(win_shape)
    return (grad_in, (d_qkv, d_proj, d_up, d_down), grad_bias)


def expand_bias(table_part, rel_index):
    return jnp.take(table_part, rel_index, axis=3)


def fold_bias(grad_bias, rel_index, n_pos):
    lead_shape = grad_bias.shape[:3]
    flat_grad = grad_bias.reshape(lead_shape + (-1,))
    empty = jnp.zeros(lead_shape + (n_pos,), jnp.float32)
    return empty.at[:, :, :, rel_index.reshape(-1)].add(flat_grad)


def roll_ahead(field, grad_field):
    arrived = passed_along((field[:, :3], grad_field[:, :3]), "lat", -1)
    field = jnp.concatenate([field[:, 3:], arrived[0]], axis=1)
    grad_field = jnp.concatenate([grad_field[:, 3:], arrived[1]], axis=1)
    arrived = passed_along((field[:, :, :6], grad_field[:, :, :6]), "lon", -1)
    field = jnp.concatenate([field[:, :, 6:], arrived[0]], axis=2)
    grad_field = jnp.concatenate([grad_field[:, :, 6:], arrived[1]], axis=2)
    return (jnp.roll(field, -1, axis=0), jnp.roll(grad_field, -1, axis=0))


def roll_back(field, grad_field):
    field = jnp.roll(field, 1, axis=0)
    grad_field = jnp.roll(grad_field, 1, axis=0)
    arrived = passed_along((field[:, :, -6:], grad_field[:, :, -6:]), "lon", 1)
    field = jnp.concatenate([arrived[0], field[:, :, :-6]], axis=2)
    grad_field = jnp.concatenate([arrived[1], grad_field[:, :, :-6]], axis=2)
    arrived = passed_along((field[:, -3:], grad_field[:, -3:]), "lat", 1)
    field = jnp.concatenate([arrived[0], field[:, :-3]], axis=1)
    grad_field = jnp.concatenate([arrived[1], grad_field[:, :-3]], axis=1)
    return (field, grad_field)


def per_device(
    tokens, grad_mixed, w_qkv, w_proj, w_up, w_down, gains, bias_table, rel_index, mask_ids
):
    levels = tokens.shape[0]
    n_pos = bias_table.shape[-1]
    weights_one = (w_qkv[0], w_proj[0], w_up[0], w_down[0], gains[0])
    weights_two = (w_qkv[1], w_proj[1], w_up[1], w_down[1], gains[1])
    bias_one = expand_bias(bias_table[0], rel_index)
    bias_two = expand_bias(bias_table[1], rel_index)
    first, saved_one = block_forward(
        to_windows(tokens), weights_one, bias_one, window_mask(levels, mask_ids, False)
    )
    shifted, grad_shifted = roll_ahead(from_windows(first), grad_mixed)
    second, saved_two = block_forward(
        to_windows(shifted), weights_two, bias_two, window_mask(levels, mask_ids, True)
    )
    grad_second, parts_two, bias_grad_two = block_backward(
        to_windows(grad_shifted), saved_two, weights_two
    )
    mixed, grad_first = roll_back(from_windows(second), from_windows(grad_second))
    grad_in, parts_one, bias_grad_one = block_backward(
        to_windows(grad_first), saved_one, weights_one
    )
    stacked = [jnp.stack([part_one, part_two]) for part_one, part_two in zip(parts_one, parts_two)]
    summed = (
        lax.psum(stacked[0].astype(jnp.bfloat16), "lat").astype(jnp.float32),
        lax.psum(stacked[1].astype(jnp.bfloat16), "lat").astype(jnp.float32),
        lax.psum(stacked[2].astype(jnp.bfloat16), "lat").astype(jnp.float32),
        lax.psum(stacked[3].astype(jnp.bfloat16), "lat").astype(jnp.float32),
    )
    reduced = (
        lax.psum_scatter(
            summed[0].astype(jnp.bfloat16), "lon", scatter_dimension=2, tiled=True
        ).astype(jnp.float32),
        lax.psum_scatter(
            summed[1].astype(jnp.bfloat16), "lon", scatter_dimension=2, tiled=True
        ).astype(jnp.float32),
        lax.psum_scatter(
            summed[2].astype(jnp.bfloat16), "lon", scatter_dimension=2, tiled=True
        ).astype(jnp.float32),
        lax.psum_scatter(
            summed[3].astype(jnp.bfloat16), "lon", scatter_dimension=2, tiled=True
        ).astype(jnp.float32),
    )
    table_local = jnp.stack(
        [fold_bias(bias_grad_one, rel_index, n_pos), fold_bias(bias_grad_two, rel_index, n_pos)]
    )
    table_grad = lax.psum(table_local.astype(jnp.bfloat16), "lon").astype(jnp.float32)
    return (
        mixed,
        from_windows(grad_in),
        reduced[0],
        reduced[1],
        reduced[2],
        reduced[3],
        table_grad,
    )


def solution(mesh):
    in_specs = (
        P(None, "lat", "lon", None),
        P(None, "lat", "lon", None),
        P(),
        P(),
        P(),
        P(),
        P(),
        P(None, None, "lat", None, None),
        P(),
        P("lat"),
    )
    out_specs = (
        P(None, "lat", "lon", None),
        P(None, "lat", "lon", None),
        P(None, None, "lon"),
        P(None, None, "lon"),
        P(None, None, "lon"),
        P(None, None, "lon"),
        P(None, None, "lat", None, None),
    )
    return jax.shard_map(
        per_device, mesh=mesh, in_specs=in_specs, out_specs=out_specs, check_vma=False
    )
```

profile of v0, /device:TPU:8, one launch (start us, length us, event | category | flops | bytes accessed | tf_op | source)
XLA Modules:
  0.0 717.2 jit_solution(9527063810653758236)
XLA Ops:
  12.2 38.9 %gather_fusion = f32[20736,6]{1,0:T(8,128)} fusion(f32[6,3312]{0,1:T(8,128)S(1)} %bitcast.246, s32[21504]{0:T(1024)S(1)} %pad_clamp_fusion), kind=kCustom, calls=%fused_computation.clone | custom fusion | bytes 1078272 | tf_op jit(solution)/shard_map/jit(_take)/gather | solution.py:152
  51.1 11.6 %copy.88 = f32[144,144,6]{0,1,2:T(8,128)S(1)} copy(f32[144,144,6]{2,1,0:T(8,128)} %bitcast.249) | data formatting | bytes 995328 | tf_op jit(solution)/shard_map/jit(_take)/gather | solution.py:152
  67.2 1.9 multiply_convert_fusion.1
  70.3 3.0 collective-permute-start
  73.4 2.3 collective-permute-start.4
  76.6 3.9 compare_select_fusion.3
  82.1 38.9 %gather_fusion.1 = f32[20736,6]{1,0:T(8,128)} fusion(f32[6,3312]{0,1:T(8,128)S(1)} %bitcast.247, s32[21504]{0:T(1024)S(1)} %pad_clamp_fusion), kind=kCustom, calls=%fused_computation.1.clone | custom fusion | bytes 1078272 | tf_op jit(solution)/shard_map/jit(_take)/gather | solution.py:152
  121.0 11.7 %copy.94 = f32[144,144,6]{0,1,2:T(8,128)S(1)} copy(f32[144,144,6]{2,1,0:T(8,128)} %bitcast.248) | data formatting | bytes 995328 | tf_op jit(solution)/shard_map/jit(_take)/gather | solution.py:152
  132.7 4.0 collective-permute-start.1
  136.8 1.5 collective-permute-start.5
  140.5 1.2 fusion.133
  142.1 2.9 multiply_convert_fusion
  148.5 1.6 add_convert_fusion.1
  151.8 1.3 subtract_multiply_fusion.1
  154.8 1.9 fusion.27
  161.8 6.2 copy.114
  168.1 112.8 %scatter_custom_fusion.1 = f32[6,3312]{0,1:T(8,128)S(1)} fusion(s32[20736]{0:T(1024)} %fusion.100, f32[20736,6]{1,0:T(8,128)} %copy.114, f32[]{:T(128)} %constant.55.clone.1), kind=kCustom, calls=%fused_computation.67 | custom fusion | flops 124416 | bytes 80000 | tf_op jit(solution)/shard_map/scatter-add | solution.py:159
  283.7 3.0 collective-permute-start.7
  287.6 1.3 copy.116
  288.9 2.4 collective-permute-done.7
  293.7 1.6 add_convert_fusion
  299.5 2.4 fusion.28
  304.0 1.4 copy.110
  306.8 1.4 copy.107
  308.8 6.2 copy.112
  315.0 112.8 %scatter_custom_fusion = f32[6,3312]{0,1:T(8,128)S(1)} fusion(s32[20736]{0:T(1024)} %fusion.100, f32[20736,6]{1,0:T(8,128)} %copy.112, f32[]{:T(128)} %constant.55.clone.1), kind=kCustom, calls=%fused_computation.69 | custom fusion | flops 124416 | bytes 80000 | tf_op jit(solution)/shard_map/scatter-add | solution.py:159
  429.7 1.8 copy.109
  435.1 2.9 collective-permute-done.2
  440.4 4.3 collective-permute-done.3
  445.4 216.9 %all-reduce.8.cloned.1.call-done = (bf16[2,192,768]{1,0,2:T(2,128)(2,1)}, bf16[2,1,1,6,3312]{4,0,3,2,1:T(2,128)(2,1)}, bf16[2,192,576]{1,0,2:T(2,128)(2,1)}, bf1...) async-done(((bf16[2,192,768]{1,0,2:T(2,128)(2,1)}, bf16[2,1,1,6,3312]{4,0,3,2,1:T(2,128)(2,1)}, bf16[2,192,576]{1,0,2:T(2,128)(2,1)}, bf16[2,192,192]{1,0,2:T(2,128)(2,1)}, ...) | async-done | bytes 1848976
  665.3 40.5 %all-reduce.5 = (bf16[2,192,24]{1,0,2:T(2,128)(2,1)S(1)}, bf16[2,192,18]{1,0,2:T(2,128)(2,1)S(1)}, bf16[2,192,6]{1,0,2:T(2,128)(2,1)S(1)}, bf16[2,768,6]{1,0,2:T(2,128)(2,1)S(1)}) all-reduce(bf16[2,192,24]{1,0,2:T(2,128)(2,1)S(1)} %constant_dynamic-slice_fusion.1, ...), channel_id=1, replica_groups=mesh['lat'=8,'lon'=32] {'lat'}, use_global_device_ids=true, to_apply=%region_26.28 | all-reduce | flops 27648 | bytes 110592 | tf_op jit(solution)/shard_map/psum | solution.py:211
  707.7 1.7 copy.119
  (291 shorter events, 53.2 us)
Async XLA Ops:
  7.2 4.3 copy-start.48
  7.2 655.1 %all-reduce.8.cloned.1.call-start = ((), (), s32[]{:S(2)}) async-start(), calls=%async_computation | async-start | bytes 4485120
  10.1 56.4 %copy-start.7 = (bf16[144,192]{1,0:T(8,128)(2,1)}, bf16[144,192]{1,0:T(8,128)(2,1)S(1)}, u32[]{:S(2)}) copy-start(bf16[144,192]{1,0:T(8,128)(2,1)S(1)} %reshape_reshape_transpose_reshape.8) | copy-start | bytes 165892
  11.5 53.0 %copy-start.4 = (bf16[144,576]{0,1:T(8,128)(2,1)}, bf16[144,576]{0,1:T(8,128)(2,1)S(1)}, u32[]{:S(2)}) copy-start(bf16[144,576]{0,1:T(8,128)(2,1)S(1)} %copy.84) | copy-start | bytes 497668
  67.2 6.1 copy-start.51
  69.1 12.4 %copy-start.16 = (bf16[144,768]{1,0:T(8,128)(2,1)}, bf16[144,768]{1,0:T(8,128)(2,1)S(1)}, u32[]{:S(2)}) copy-start(bf16[144,768]{1,0:T(8,128)(2,1)S(1)} %get-tuple-element.50) | copy-start | bytes 663556
  69.1 6.6 copy-start.6
  69.2 6.8 copy-start.56
  70.3 62.3 %collective-permute-start = (bf16[2,3,12,192]{3,2,1,0:T(8,128)(2,1)S(1)}, bf16[2,3,12,192]{3,2,1,0:T(8,128)(2,1)S(1)}, u32[]{:S(2)}, u32[]{:S(2)}) collective-permute-start(bf16[2,3,12,192]{3,2,1,0:T(8,128)(2,1)S(1)} %get-tuple-element.60), channel_id=1, source_target_pairs={{0,224},{32,0},{64,32},{96,64},{128,96},{160,128},{192,160},{224,1... | collective-permute-start | bytes 82952 | tf_op jit(solution)/shard_map/ppermute | solution.py:16
  73.4 63.3 %collective-permute-start.4 = (bf16[2,3,12,192]{3,0,2,1:T(2,128)(2,1)S(1)}, bf16[2,3,12,192]{3,0,2,1:T(2,128)(2,1)S(1)}, u32[]{:S(2)}, u32[]{:S(2)}) collective-permute-start(bf16[2,3,12,192]{3,0,2,1:T(2,128)(2,1)S(1)} %get-tuple-element.70), channel_id=1, source_target_pairs={{0,224},{32,0},{64,32},{96,64},{128,96},{160,128},{192,160},{224,1... | collective-permute-start | bytes 82952 | tf_op jit(solution)/shard_map/ppermute | solution.py:16
  121.0 17.6 %copy-start.3 = (bf16[2,192,576]{2,1,0:T(8,128)(2,1)S(1)}, bf16[2,192,576]{2,1,0:T(8,128)(2,1)}, u32[]{:S(2)}) copy-start(bf16[2,192,576]{2,1,0:T(8,128)(2,1)} %param.14) | copy-start | bytes 1327108
  132.7 5.7 collective-permute-start.1
  136.8 8.6 %collective-permute-start.5 = (bf16[2,6,6,192]{3,0,2,1:T(2,128)(2,1)S(1)}, bf16[2,6,6,192]{3,0,2,1:T(2,128)(2,1)S(1)}, u32[]{:S(2)}, u32[]{:S(2)}) collective-permute-start(bf16[2,6,6,192]{3,0,2,1:T(2,128)(2,1)S(1)} %get-tuple-element.68), channel_id=1, source_target_pairs={{0,31},{1,0},{2,1},{3,2},{4,3},{5,4},{6,5},{7,6},{8,7},{9,8},{10,9... | collective-permute-start | bytes 82952 | tf_op jit(solution)/shard_map/ppermute | solution.py:16
  140.2 11.0 %copy-start.2 = (f32[6,144,144]{1,2,0:T(8,128)}, f32[6,144,144]{1,2,0:T(8,128)S(1)}, u32[]{:S(2)}) copy-start(f32[6,144,144]{1,2,0:T(8,128)S(1)} %get-tuple-element.91) | copy-start | bytes 1492996
  140.5 4.6 copy-start.42
  142.1 5.6 copy-start.23
  161.3 121.7 %collective-permute-start.6 = (bf16[2,6,6,192]{3,2,1,0:T(8,128)(2,1)}, bf16[2,6,6,192]{3,2,1,0:T(8,128)(2,1)}, u32[]{:S(2)}, u32[]{:S(2)}) collective-permute-start(bf16[2,6,6,192]{3,2,1,0:T(8,128)(2,1)} %get-tuple-element.55), channel_id=1, source_target_pairs={{0,1},{1,2},{2,3},{3,4},{4,5},{5,6},{6,7},{7,8},{8,9},{9,10},{10,1... | collective-permute-start | bytes 82952 | tf_op jit(solution)/shard_map/ppermute | solution.py:16
  280.9 5.8 copy-start.43
  281.9 9.4 %copy-start.35 = (bf16[2,6,6,192]{3,2,1,0:T(8,128)(2,1)S(1)}, bf16[2,6,6,192]{3,2,1,0:T(8,128)(2,1)}, u32[]{:S(2)}) copy-start(bf16[2,6,6,192]{3,2,1,0:T(8,128)(2,1)} %get-tuple-element.56) | copy-start | bytes 82948
  281.9 10.2 %copy-start.55 = (f32[144]{0:T(256)S(1)}, f32[144]{0:T(256)}, u32[]{:S(2)}) copy-start(f32[144]{0:T(256)} %copy-done.54) | copy-start | bytes 1732
  281.9 10.2 %copy-start.60 = (f32[1,1,192]{2,1,0:T(1,128)S(1)}, f32[1,1,192]{2,1,0:T(1,128)}, u32[]{:S(2)}) copy-start(f32[1,1,192]{2,1,0:T(1,128)} %copy-done.59) | copy-start | bytes 2308
  281.9 10.4 %copy-start.70 = (f32[144]{0:T(256)S(1)}, f32[144]{0:T(256)}, u32[]{:S(2)}) copy-start(f32[144]{0:T(256)} %copy-done.69) | copy-start | bytes 1732
  281.9 10.4 %copy-start.65 = (f32[144]{0:T(256)S(1)}, f32[144]{0:T(256)}, u32[]{:S(2)}) copy-start(f32[144]{0:T(256)} %copy-done.64) | copy-start | bytes 1732
  281.9 10.7 %copy-start.17 = (bf16[144,768]{1,0:T(8,128)(2,1)S(1)}, bf16[144,768]{1,0:T(8,128)(2,1)}, u32[]{:S(2)}) copy-start(bf16[144,768]{1,0:T(8,128)(2,1)} %copy-done.16) | copy-start | bytes 663556
  283.7 10.0 %copy-start.73 = (f32[144,768]{1,0:T(8,128)S(1)}, f32[144,768]{1,0:T(8,128)}, u32[]{:S(2)}) copy-start(f32[144,768]{1,0:T(8,128)} %get-tuple-element.51) | copy-start | bytes 1327108
  283.7 7.5 %collective-permute-start.7 = (bf16[2,3,12,192]{3,2,1,0:T(8,128)(2,1)S(1)}, bf16[2,3,12,192]{3,2,1,0:T(8,128)(2,1)S(1)}, u32[]{:S(2)}, u32[]{:S(2)}) collective-permute-start(bf16[2,3,12,192]{3,2,1,0:T(8,128)(2,1)S(1)} %fusion.104), channel_id=1, source_target_pairs={{0,32},{32,64},{64,96},{96,128},{128,160},{160,192},{192,224},{224... | collective-permute-start | bytes 82952 | tf_op jit(solution)/shard_map/ppermute | solution.py:16
  293.7 3.5 copy-start.1
  293.7 3.5 copy-start.5
  293.7 3.5 copy-start.53
  427.9 3.6 copy-start.46
  432.5 5.6 collective-permute-start.2
  438.3 6.4 collective-permute-start.3
  (51 other events, 103.3 us)
Sparse Core Ops, SparseCore 0:
  432.4 229.8 all-reduce.7
where the time goes:
time: 728 us; the launch traced here: 717 us
  other arithmetic  247 us (34%)
  waiting for transfers between devices  227 us (31%)
  local copies, waits for them, and re-layouts  140 us (19%)
  blocking collectives  40.5 us (6%)
  matrix products  30.5 us (4%)
  between operations  17.6 us (2%)
  starting transfers between devices  15.1 us (2%)
    scatter-add x2, other arithmetic, fold_bias(): return empty.at[:, :, :, rel_index.reshape(-1)].add(flat_grad)  226 us
    unnamed x2, waiting for transfers between devices  217 us
    gather x4, local copies, waits for them, and re-layouts, expand_bias(): return jnp.take(table_part, rel_index, axis=3)  101 us
    psum x1, blocking collectives, per_device(): lax.psum(stacked[2].astype(jnp.bfloat16), 'lat').astype(jnp.float32)  40.5 us
    ppermute x8, starting transfers between devices, passed_along(): return lax.ppermute(value, axis, pairs)  15.1 us
  transfers between devices with their start and end apart: 9, of which 5 were waited for; matrix products, arithmetic and copies ran while one was open for 26% of the time, Pallas kernels for 0%

commit v1 on v0

v1 whole, which is shorter than its diff:
```python
import functools

import jax
import jax.numpy as jnp
import numpy as np
from jax import lax
from jax.experimental import pallas as pl
from jax.experimental.pallas import tpu as pltpu
from jax.sharding import PartitionSpec as P

HEADS = 6
C = 192
TOK = 144
POS = 3312
EPS = 1e-05
NEGATIVE = -1e30
SCALE = 32 ** -0.5
BF = jnp.bfloat16
F32 = jnp.float32
MESH = pl.DeviceIdType.MESH
ROWS = 168
TAIL = 144
N_SEMS = 92


def index_rows():
    rows = np.full((16, 768), -1, np.int32)
    tok = np.arange(TOK)
    level, row, col = tok // 72, tok // 12 % 6, tok % 12
    place = 24 * row + 2 * col + level
    own = 18 * level + row % 3 * 6 + col % 6
    other = 18 * (1 - level) + row % 3 * 6 + col % 6
    low = 48 * (2 * (row // 3) + col // 6)
    high = 48 * (2 * (1 - row // 3) + 1 - col // 6)
    rows[0, place] = tok
    rows[1, tok] = place
    rows[2, tok] = high + own
    rows[3, low + other] = tok
    rows[4, tok] = low + own
    rows[5, high + other] = tok
    rows[6, high + other] = place
    rows[10, place] = high + own
    for piece in range(32):
        for i in range(18):
            rows[7, 24 * piece + i] = 18 * piece + i
        for i in range(6):
            rows[8, 24 * piece + 18 + i] = 6 * piece + i
            rows[9, 8 * piece + i] = 6 * piece + i
    return rows


def dot(a, b):
    return jnp.dot(a, b, preferred_element_type=F32)


def dot_nt(a, b):
    return lax.dot_general(a, b, (((1,), (1,)), ((), ())), preferred_element_type=F32)


def dot_tn(a, b):
    return lax.dot_general(a, b, (((0,), (0,)), ((), ())), preferred_element_type=F32)


def norm_parts(v):
    center = v - jnp.mean(v, axis=-1, keepdims=True)
    spread = jnp.mean(center * center, axis=-1, keepdims=True)
    inverse = lax.rsqrt(spread + EPS)
    return center * inverse, inverse


def norm_back(grad, unit, inverse):
    along = jnp.mean(grad * unit, axis=-1, keepdims=True)
    return inverse * (grad - jnp.mean(grad, axis=-1, keepdims=True) - unit * along)


def kernel(
    n_lat, n_lon,
    rel_hbm, table_hbm, const_hbm, tok_hbm, gmix_hbm, wqkv_hbm, wproj_hbm, gains_hbm, wup_hbm, wdown_hbm, ids_ref,
    mixed_ref, gtok_ref, wg_ref, tgrad_ref,
    rel_ref, table_ref, const_ref, tok_ref, gmix_ref, wqkv_ref, wproj_ref, gains_ref, wup_ref, wdown_ref, load_sem,
    x_ref, qkv_ref, qm_ref, s_ref, p_ref, att_ref, u1_ref, i1_ref, mid_ref, gp_ref, hid_ref, u2_ref, i2_ref,
    gup_ref, gam_ref, ds_ref, idx_ref, low_ref, oht_ref, tabf_ref, tab_ref, bias_ref, btail_ref, pk_ref, gall_ref, acc_ref,
    l_ref, r_ref, o1_ref, o3_ref,
    hs_ref, hr_ref,
    sb_ref, rc_ref, wa_ref, rx_ref, wc_ref, rz_ref, wd_ref, wl_ref,
    tb_ref, tr1_ref, t1_ref, tr2_ref, t2_ref, t3_ref, t4_ref,
    ssem, rsem,
):
    loads = [
        pltpu.make_async_copy(src, dst, load_sem.at[k])
        for k, (src, dst) in enumerate([
            (rel_hbm, rel_ref), (table_hbm, table_ref), (const_hbm, const_ref), (tok_hbm, tok_ref), (gmix_hbm, gmix_ref),
            (wqkv_hbm, wqkv_ref), (wproj_hbm, wproj_ref), (gains_hbm, gains_ref), (wup_hbm, wup_ref), (wdown_hbm, wdown_ref),
        ])
    ]
    for load in loads:
        load.start()
    ny, nz = n_lat // 2, n_lon // 4
    lat, lon = lax.axis_index("lat"), lax.axis_index("lon")
    y, xh = lat // 2, lat % 2
    z, xl, co = lon // 4, lon // 2 % 2, lon % 2
    x = xh * 2 + xl
    lon_pair = [
        (z * 4 + ((xl + (k >> 1)) % 2) * 2 + (co + (k & 1)) % 2, (xl + (k >> 1)) % 2, (co + (k & 1)) % 2)
        for k in range(4)
    ]
    ahead = [((lat + n_lat - a) % n_lat, (lon + n_lon - b) % n_lon) for a in (0, 1) for b in (0, 1)]
    back = [((lat + a) % n_lat, (lon + b) % n_lon) for a in (0, 1) for b in (0, 1)]
    z_lons = [(z + k) % nz * 4 + xl * 2 + co for k in range(nz)]

    greeted = [((lat + k) % n_lat, lon) for k in range(1, n_lat)]
    greeted += [(lat, z_lons[k]) for k in range(1, nz)]
    greeted += [(lat, lon_pair[k][0]) for k in (1, 3)]
    greeted += [((lat + k) % n_lat, lon_pair[2][0]) for k in range(n_lat)]
    greeted += [ahead[1], ahead[3], back[1], back[3]]
    barrier = pltpu.get_barrier_semaphore()
    for device in greeted:
        pl.semaphore_signal(barrier, inc=1, device_id=device, device_id_type=MESH)

    sems = iter(range(N_SEMS))
    sent = []

    def push(src, dst, device):
        k = next(sems)
        copy = pltpu.make_async_remote_copy(
            src_ref=src, dst_ref=dst, send_sem=ssem.at[k], recv_sem=rsem.at[k], device_id=device, device_id_type=MESH
        )
        copy.start()
        sent.append(copy)
        return copy

    def arrive(copies):
        for copy in copies:
            copy.wait_recv()

    def onehot(n_rows, n_lanes, which):
        place = lax.broadcasted_iota(jnp.int32, (n_rows, n_lanes), 0)
        return jnp.where(place == const_ref[which : which + 1, :n_lanes], 1.0, 0.0).astype(BF)

    def moved(matrix, value):
        return dot(matrix, value).astype(BF)

    lane = lax.broadcasted_iota(jnp.int32, (1, C), 1)
    head_lanes = [(lane >= 32 * h) & (lane < 32 * h + 32) for h in range(HEADS)]

    def of_head(value, h):
        return jnp.where(head_lanes[h], value, jnp.zeros_like(value))

    def pack_tail(value, h):
        pk_ref[h, 0:TOK, 0:16] = value
        total = pk_ref[h, pl.ds(0, 24, stride=8), :]
        for j in range(1, 8):
            total = total + pltpu.roll(pk_ref[h, pl.ds(j, 24, stride=8), :], 16 * j, 1)
        return total

    def unpack_tail(value, k):
        for j in range(8):
            rolled = pltpu.roll(value, (128 - 16 * j) % 128, 1)
            btail_ref[k, pl.ds(j, 24, stride=8), :] = rolled

    def gather_biases():
        place = lax.broadcasted_iota(jnp.int32, (256, 128), 0).astype(BF)
        one, zero = jnp.ones((256, 128), BF), jnp.zeros((256, 128), BF)

        def step(i, carry):
            index = idx_ref[pl.ds(pl.multiple_of(i * 8, 8), 8), :]
            low, high = (index & 255).astype(F32), index >> 8
            picks = []
            for r in range(8):
                row = jnp.broadcast_to(low[r : r + 1, :], (16, 128)).astype(BF)
                picks.append(jnp.where(place == jnp.concatenate([row] * 16, axis=0), one, zero))
            rows = dot(tab_ref[...], jnp.concatenate(picks, axis=1))
            for r in range(8):
                high_row = jnp.broadcast_to(high[r : r + 1, :], (16, 128))
                found = jnp.zeros((16, 128), F32)
                for part in range(13):
                    coarse = rows[16 * part : 16 * part + 16, 128 * r : 128 * r + 128]
                    fine = rows[208 + 16 * part : 224 + 16 * part, 128 * r : 128 * r + 128]
                    found = jnp.where(high_row == part, coarse + fine, found)
                bias_ref[pl.ds(pl.multiple_of(i * 128 + r * 16, 16), 16), :] = found
            return carry

        lax.fori_loop(0, ROWS // 8, step, 0)
        for b in range(2):
            for h in range(HEADS):
                unpack_tail(bias_ref[pl.ds(16 * TAIL + 8 * b + h, 24, stride=16), :], 6 * b + h)

    def expand_index():
        place = lax.broadcasted_iota(jnp.int32, (128, 256), 1).astype(BF)
        one, zero = jnp.ones((128, 256), BF), jnp.zeros((128, 256), BF)

        def step(i, carry):
            block = low_ref[i]
            for r in range(8):
                span = pl.ds(pl.multiple_of(i * 1024 + r * 128, 128), 128)
                column = jnp.broadcast_to(block[:, r : r + 1], (128, 128)).astype(BF)
                oht_ref[span, :] = jnp.where(place == jnp.concatenate([column] * 2, axis=1), one, zero)
            return carry

        lax.fori_loop(0, ROWS // 8, step, 0)

    def fold_tables():
        acc_ref[...] = jnp.zeros_like(acc_ref)

        def step(i, carry):
            high = idx_ref[pl.ds(pl.multiple_of(i * 8, 8), 8), :] >> 8
            left = [[] for _ in range(26)]
            for r in range(8):
                high_row = jnp.broadcast_to(high[r : r + 1, :], (8, 128))
                for b in range(2):
                    grads = gall_ref[b, pl.ds(pl.multiple_of(i * 64 + r * 8, 8), 8), :]
                    for part in range(13):
                        left[13 * b + part].append(jnp.where(high_row == part, grads, 0.0))
            left = jnp.concatenate([jnp.concatenate(rows, axis=1) for rows in left], axis=0).astype(BF)
            acc_ref[...] += dot(left, oht_ref[pl.ds(pl.multiple_of(i * 1024, 1024), 1024), :])
            return carry

        lax.fori_loop(0, ROWS // 8, step, 0)

    def region_codes(place):
        code = jnp.zeros_like(place)
        for part in range(12):
            value = ids_ref[part % 6] + 64 * (part // 6)
            code = jnp.where(place >= 12 * part, value, code)
        return code

    def forward(b):
        tokens = x_ref[b]
        qkv_ref[b] = dot(tokens, wqkv_ref[b]).astype(BF)
        q, k, v = (qkv_ref[b, :, C * i : C * i + C] for i in range(3))
        for h in range(HEADS):
            qm_ref[b, TOK * h : TOK * h + TOK, :] = of_head(q, h)
        s_ref[...] = dot_nt(qm_ref[b], k)
        if b == 1:
            codes_s = region_codes(lax.broadcasted_iota(jnp.int32, (TOK, 1), 0))
            codes_t = region_codes(lax.broadcasted_iota(jnp.int32, (1, TOK), 1))
            allowed = codes_s == codes_t
        for h in range(HEADS):
            span = pl.ds(TOK * h, TOK)
            main = bias_ref[pl.ds(8 * b + h, TOK, stride=16), :]
            bias = jnp.concatenate([main, btail_ref[6 * b + h, 0:TOK, 0:16]], axis=1)
            scores = s_ref[span, :] * SCALE + bias
            if b == 1:
                scores = jnp.where(allowed, scores, NEGATIVE)
            powers = jnp.exp(scores - jnp.max(scores, axis=-1, keepdims=True))
            probs = powers * (1.0 / jnp.sum(powers, axis=-1, keepdims=True))
            p_ref[b, span, :] = probs.astype(BF)
        attended = jnp.zeros((TOK, C), F32)
        for h in range(HEADS):
            attended = jnp.where(head_lanes[h], dot(p_ref[b, TOK * h : TOK * h + TOK, :], v), attended)
        attended = attended.astype(BF)
        att_ref[b] = attended
        unit, inverse = norm_parts(dot(attended, wproj_ref[b]))
        u1_ref[b], i1_ref[b] = unit, inverse
        middle = (tokens.astype(F32) + unit * gains_ref[b, 0:1, :]).astype(BF)
        mid_ref[b] = middle
        for part in range(3):
            cols = pl.ds(256 * part, 256)
            up = dot(middle, wup_ref[b, :, cols])
            phi = 0.5 + 0.5 * lax.erf(up * (0.5**0.5))
            hid_ref[b, :, cols] = (up * phi).astype(BF)
            gp_ref[b, :, cols] = phi + up * (0.3989422804014327 * jnp.exp(-0.5 * up * up))
        unit, inverse = norm_parts(dot_nt(hid_ref[b], wdown_ref[b]))
        u2_ref[b], i2_ref[b] = unit, inverse
        return (middle.astype(F32) + unit * gains_ref[b, 1:2, :]).astype(BF)

    def backward(b, grad, between):
        grad = grad.astype(F32)
        grad_down = norm_back(grad * gains_ref[b, 1:2, :], u2_ref[b], i2_ref[b]).astype(BF)
        for part in range(3):
            cols = pl.ds(256 * part, 256)
            grad_hidden = dot(grad_down, wdown_ref[b, :, cols])
            gup_ref[b, :, cols] = (grad_hidden * gp_ref[b, :, cols]).astype(BF)
        grad_middle = grad + dot_nt(gup_ref[b], wup_ref[b])
        between()
        grad_pre = norm_back(grad_middle * gains_ref[b, 0:1, :], u1_ref[b], i1_ref[b]).astype(BF)
        grad_att = dot_nt(grad_pre, wproj_ref[b]).astype(BF)
        for h in range(HEADS):
            gam_ref[TOK * h : TOK * h + TOK, :] = of_head(grad_att, h)
        q, k, v = (qkv_ref[b, :, C * i : C * i + C] for i in range(3))
        s_ref[...] = dot_nt(gam_ref[...], v)
        between()
        for h in range(HEADS):
            span = pl.ds(TOK * h, TOK)
            probs = p_ref[b, span, :].astype(F32)
            grad_probs = s_ref[span, :]
            grad_scores = probs * (grad_probs - jnp.sum(grad_probs * probs, axis=-1, keepdims=True))
            ds_ref[span, :] = grad_scores.astype(BF)
            gall_ref[b, pl.ds(h, TOK, stride=8), :] = grad_scores[:, 0:128]
            gall_ref[b, pl.ds(8 * TAIL + h, 24, stride=8), :] = pack_tail(grad_scores[:, 128:TOK], h)
        between()
        grad_q = jnp.zeros((TOK, C), F32)
        for h in range(HEADS):
            grad_q = jnp.where(head_lanes[h], dot(ds_ref[TOK * h : TOK * h + TOK, :], k), grad_q)
        grad_k = dot_tn(ds_ref[...], qm_ref[b])
        grad_v = dot_tn(p_ref[b], gam_ref[...])
        grad_qkv = jnp.concatenate([grad_q * SCALE, grad_k * SCALE, grad_v], axis=1).astype(BF)
        grad_in = (grad_middle + dot_nt(grad_qkv, wqkv_ref[b])).astype(BF)
        return grad_in, grad_down, grad_pre, grad_qkv

    def weight_grads(b, grad_down, grad_pre, grad_qkv):
        l_ref[0:TOK, :] = moved(grad_qkv, onehot(3 * C, 768, 7))
        l_ref[TOK : 2 * TOK, :] = moved(grad_pre, onehot(C, 768, 8))
        l_ref[2 * TOK : 3 * TOK, :] = gup_ref[b]
        tokens, middle = x_ref[b], mid_ref[b]
        r_ref[0:TOK, 0:128] = tokens[:, 0:128]
        r_ref[0:TOK, 256:320] = tokens[:, 128:C]
        r_ref[TOK : 2 * TOK, 0:128] = att_ref[b, :, 0:128]
        r_ref[TOK : 2 * TOK, 256:320] = att_ref[b, :, 128:C]
        r_ref[2 * TOK : 3 * TOK, 128:256] = middle[:, 0:128]
        r_ref[2 * TOK : 3 * TOK, 320:384] = middle[:, 128:C]
        o1_ref[...] = dot_tn(l_ref[...], r_ref[...])
        o3_ref[...] = dot_tn(moved(grad_down, onehot(C, 256, 9)), hid_ref[b])
        rows = 128 // n_lat
        for piece in range(32):
            units = [o1_ref[24 * piece + 8 * i : 24 * piece + 8 * i + 8, 128 * m : 128 * m + 128] for m in range(3) for i in range(3)]
            units += [o3_ref[8 * piece : 8 * piece + 8, 128 * i : 128 * i + 128] for i in range(6)]
            units += [jnp.zeros((8, 128), F32)]
            for tile in range(8):
                pair = jnp.concatenate([units[2 * tile], units[2 * tile + 1]], axis=0).astype(BF)
                at, off = 16 * tile // rows, 16 * tile % rows
                across = at % 2 * 2 + piece // 2 % 2
                sb_ref[b, piece % 2, at // 2, across, piece // 4, off : off + 16, :] = pair

    class Sum:
        def __init__(self, b):
            self.b = b
            self.copies = []
            self.steps = [self.core, self.along_xy, self.along_z, self.share, self.done]

        def next(self):
            if self.steps:
                self.steps.pop(0)()

        def core(self):
            self.copies = [push(sb_ref.at[self.b, 1 - co], rc_ref.at[self.b], (lat, lon + 1 - 2 * co))]

        def along_xy(self):
            b = self.b
            arrive(self.copies)
            wa_ref[b] = (sb_ref[b, co].astype(F32) + rc_ref[b].astype(F32)).astype(BF)
            self.copies = []
            for k in range(1, 4 * ny):
                its_y, its_x = (y + k // 4) % ny, (x + k % 4) % 4
                device = (its_y * 2 + its_x // 2, z * 4 + its_x % 2 * 2 + co)
                self.copies.append(push(wa_ref.at[b, its_y, its_x], rx_ref.at[b, k - 1], device))

        def along_z(self):
            b = self.b
            arrive(self.copies)
            total = wa_ref[b, y, x].astype(F32)
            for k in range(4 * ny - 1):
                total = total + rx_ref[b, k].astype(F32)
            wc_ref[b] = total.astype(BF)
            self.copies = []
            for k in range(1, nz):
                self.copies.append(push(wc_ref.at[b, (z + k) % nz], rz_ref.at[b, k - 1], (lat, z_lons[k])))

        def share(self):
            b = self.b
            arrive(self.copies)
            total = wc_ref[b, z].astype(F32)
            for k in range(nz - 1):
                total = total + rz_ref[b, k].astype(F32)
            wd_ref[b] = total.astype(BF)
            self.copies = []
            for k in range(1, n_lat):
                self.copies.append(push(wd_ref.at[b], wl_ref.at[b, lat], ((lat + k) % n_lat, lon)))
            wl_ref[b, lat] = wd_ref[b]

        def done(self):
            arrive(self.copies)
            wg_ref[self.b] = wl_ref[self.b]

    class TableSum:
        def __init__(self):
            self.copies = []
            self.steps = [self.pair, self.along_z, self.share_z, self.share_pair, self.done]

        def next(self):
            if self.steps:
                self.steps.pop(0)()

        def pair(self):
            for part in range(26):
                row, lanes = 8 * (part // 2), slice(128 * (part % 2), 128 * (part % 2) + 128)
                both = jnp.concatenate([acc_ref[row : row + 8, lanes], acc_ref[104 + row : 112 + row, lanes]], axis=0)
                tb_ref[part // 16, part // 8 % 2, part % 8] = both.astype(BF)
            for part in range(26, 32):
                tb_ref[part // 16, part // 8 % 2, part % 8] = jnp.zeros((16, 128), BF)
            for k in range(1, 4):
                device, its_xl, its_co = lon_pair[k]
                self.copies.append(push(tb_ref.at[its_co, its_xl], tr1_ref.at[k - 1], (lat, device)))

        def along_z(self):
            arrive(self.copies)
            total = tb_ref[co, xl].astype(F32)
            for k in range(3):
                total = total + tr1_ref[k].astype(F32)
            t1_ref[...] = total.astype(BF)
            self.copies = []
            for k in range(1, nz):
                self.copies.append(push(t1_ref.at[(z + k) % nz], tr2_ref.at[k - 1], (lat, z_lons[k])))

        def share_z(self):
            arrive(self.copies)
            total = t1_ref[z].astype(F32)
            for k in range(nz - 1):
                total = total + tr2_ref[k].astype(F32)
            t2_ref[...] = total.astype(BF)
            self.copies = []
            for k in range(1, nz):
                self.copies.append(push(t2_ref, t3_ref.at[z], (lat, z_lons[k])))
            t3_ref[z] = t2_ref[...]

        def share_pair(self):
            arrive(self.copies)
            self.copies = []
            for k in range(1, 4):
                self.copies.append(push(t3_ref, t4_ref.at[co, xl], (lat, lon_pair[k][0])))
            t4_ref[co, xl] = t3_ref[...]

        def done(self):
            arrive(self.copies)
            tgrad_ref[...] = t4_ref[...]

    def send_quarters(which, devices):
        copies = []
        for quarter in range(1, 4):
            copies.append(push(hs_ref.at[which, quarter], hr_ref.at[which, quarter], devices[quarter]))
        hr_ref[which, 0] = hs_ref[which, 0]
        return copies

    pk_ref[...] = jnp.zeros_like(pk_ref)
    gall_ref[...] = jnp.zeros_like(gall_ref)
    r_ref[...] = jnp.zeros_like(r_ref)
    loads[0].wait()
    idx_ref[0:TOK, :] = rel_ref[:, 0:128]
    idx_ref[TAIL:ROWS, :] = pack_tail(rel_ref[:, 128:TOK].astype(F32), 0).astype(jnp.int32)
    idx_ref[TAIL + 18 : ROWS, :] = jnp.full((ROWS - TAIL - 18, 128), -1, jnp.int32)
    low = (idx_ref[...] & 255).astype(F32).T
    for i in range(ROWS // 8):
        low_ref[i] = low[:, 8 * i : 8 * i + 8]
    loads[1].wait()
    tabf_ref[...] = jnp.zeros_like(tabf_ref)
    for b in range(2):
        for part in range(13):
            width = min(256, POS - 256 * part)
            tabf_ref[16 * part + 8 * b : 16 * part + 8 * b + 6, 0:width] = table_ref[
                6 * b : 6 * b + 6, 0, 256 * part : 256 * part + width
            ]
    table = tabf_ref[...]
    coarse = table.astype(BF)
    tab_ref[0:208, :] = coarse
    tab_ref[208:416, :] = (table - coarse.astype(F32)).astype(BF)
    gather_biases()
    for load in loads[2:]:
        load.wait()
    x_ref[0] = moved(onehot(TOK, TOK, 0), tok_ref[...].reshape(TOK, C))
    hs_ref[0] = moved(onehot(192, TOK, 10), gmix_ref[...].reshape(TOK, C)).reshape(4, 48, C)

    first = forward(0)
    hs_ref[1] = moved(onehot(192, TOK, 2), first).reshape(4, 48, C)
    pl.semaphore_wait(barrier, len(greeted))
    copies_x = send_quarters(1, ahead)
    copies_g = send_quarters(0, ahead)
    expand_index()
    arrive(copies_x)
    arrive(copies_g)
    come = onehot(TOK, 192, 3)
    x_ref[1] = moved(come, hr_ref[1].reshape(192, C))
    grad_shifted = moved(come, hr_ref[0].reshape(192, C))

    second = forward(1)
    hs_ref[2] = moved(onehot(192, TOK, 4), second).reshape(4, 48, C)
    grad_second, *rest = backward(1, grad_shifted, lambda: None)
    hs_ref[3] = moved(onehot(192, TOK, 4), grad_second).reshape(4, 48, C)
    copies_s = send_quarters(3, back)
    copies_m = send_quarters(2, back)
    weight_grads(1, *rest)
    sum_two = Sum(1)
    sum_two.next()

    arrive(copies_s)
    grad_first = moved(onehot(TOK, 192, 5), hr_ref[3].reshape(192, C))
    grad_in, *rest = backward(0, grad_first, sum_two.next)
    weight_grads(0, *rest)
    sum_one = Sum(0)
    sum_one.next()
    sum_one.next()
    fold_tables()
    sum_table = TableSum()
    sum_table.next()
    arrive(copies_m)
    mixed_ref[...] = moved(onehot(TOK, 192, 6), hr_ref[2].reshape(192, C)).reshape(72, 2, C)
    gtok_ref[...] = moved(onehot(TOK, TOK, 1), grad_in).reshape(72, 2, C)
    for _ in range(5):
        sum_one.next()
        sum_table.next()
        sum_two.next()
    for copy in sent:
        copy.wait_send()


def finish(mixed_in, gtok_in, wg_in, table_in, mixed_ref, gtok_ref, qkv_ref, proj_ref, up_ref, down_ref, table_ref):
    mixed_ref[...] = mixed_in[...]
    gtok_ref[...] = gtok_in[...]
    for b in range(2):
        rows = wg_in[b].reshape(128, 128).astype(F32)
        qkv_ref[:, b, 0:128] = rows[0:18, :]
        qkv_ref[:, b, 128:C] = rows[48:66, 0:64]
        proj_ref[:, b, 0:128] = rows[18:24, :]
        proj_ref[:, b, 128:C] = rows[66:72, 0:64]
        up_ref[b, :, 0:128] = rows[24:48, :]
        up_ref[b, :, 128:C] = rows[48:72, 64:128]
        for i in range(6):
            down_ref[:, b, 128 * i : 128 * i + 128] = rows[72 + 8 * i : 78 + 8 * i, :]
    for part in range(26):
        tile = table_in[part // 16, part // 8 % 2, part % 8].astype(F32)
        width = min(128, POS - 128 * part)
        for b in range(2):
            table_ref[6 * b : 6 * b + 6, 0, 128 * part : 128 * part + width] = tile[8 * b : 8 * b + 6, 0:width]


def per_device(tokens, grad_mixed, w_qkv, w_proj, w_up, w_down, gains, bias_table, rel_index, mask_ids):
    n_lat, n_lon = lax.axis_size("lat"), lax.axis_size("lon")
    ny, nz, rows = n_lat // 2, n_lon // 4, 128 // n_lat
    vmem = pl.BlockSpec(memory_space=pltpu.VMEM)
    smem = pl.BlockSpec(memory_space=pltpu.SMEM)

    def buf(*shape, dtype=BF):
        return pltpu.VMEM(shape, dtype)

    scratch = [
        buf(TOK, TOK, dtype=jnp.int32), buf(12, 1, POS, dtype=F32), buf(16, 768, dtype=jnp.int32),
        buf(72, 2, C), buf(72, 2, C), buf(2, C, 3 * C), buf(2, C, C), buf(2, 2, C, dtype=F32), buf(2, C, 768), buf(2, C, 768),
        pltpu.SemaphoreType.DMA((10,)),
        buf(2, TOK, C), buf(2, TOK, 3 * C), buf(2, 6 * TOK, C), buf(6 * TOK, TOK, dtype=F32),
        buf(2, 6 * TOK, TOK), buf(2, TOK, C), buf(2, TOK, C, dtype=F32), buf(2, TOK, 1, dtype=F32), buf(2, TOK, C),
        buf(2, TOK, 768, dtype=F32), buf(2, TOK, 768), buf(2, TOK, C, dtype=F32), buf(2, TOK, 1, dtype=F32),
        buf(2, TOK, 768), buf(6 * TOK, C), buf(6 * TOK, TOK),
        buf(ROWS, 128, dtype=jnp.int32), buf(ROWS // 8, 128, 8, dtype=F32), buf(128 * ROWS, 256), buf(208, 256, dtype=F32),
        buf(416, 256), buf(16 * ROWS, 128, dtype=F32), buf(12, 192, 128, dtype=F32), buf(6, 192, 128, dtype=F32),
        buf(2, 8 * ROWS, 128, dtype=F32), buf(208, 256, dtype=F32),
        buf(3 * TOK, 768), buf(3 * TOK, 384), buf(768, 384, dtype=F32), buf(256, 768, dtype=F32),
        buf(4, 4, 48, C), buf(4, 4, 48, C),
        buf(2, 2, ny, 4, nz, rows, 128), buf(2, ny, 4, nz, rows, 128), buf(2, ny, 4, nz, rows, 128),
        buf(2, 4 * ny - 1, nz, rows, 128),
        buf(2, nz, rows, 128), buf(2, nz - 1, rows, 128), buf(2, rows, 128), buf(2, n_lat, rows, 128),
        buf(2, 2, 8, 16, 128), buf(3, 8, 16, 128), buf(8, 16, 128), buf(7, 16, 128), buf(16, 128),
        buf(8, 16, 128), buf(2, 2, 8, 16, 128),
        pltpu.SemaphoreType.DMA((N_SEMS,)), pltpu.SemaphoreType.DMA((N_SEMS,)),
    ]
    results = pl.pallas_call(
        functools.partial(kernel, n_lat, n_lon),
        out_shape=(
            jax.ShapeDtypeStruct((72, 2, C), BF),
            jax.ShapeDtypeStruct((72, 2, C), BF),
            jax.ShapeDtypeStruct((2, n_lat, rows, 128), BF),
            jax.ShapeDtypeStruct((2, 2, 8, 16, 128), BF),
        ),
        in_specs=[pl.BlockSpec(memory_space=pltpu.HBM)] * 10 + [smem],
        out_specs=[vmem] * 4,
        scratch_shapes=scratch,
        compiler_params=pltpu.CompilerParams(
            collective_id=0, has_side_effects=True, vmem_limit_bytes=60 * 1024 * 1024
        ),
    )(
        rel_index,
        bias_table.reshape(12, 1, POS),
        jnp.asarray(index_rows()),
        tokens.transpose(1, 2, 0, 3).reshape(72, 2, C),
        grad_mixed.transpose(1, 2, 0, 3).reshape(72, 2, C),
        w_qkv, w_proj, gains, w_up, w_down.transpose(0, 2, 1),
        mask_ids,
    )
    mixed, grad_tokens, qkv, proj, up, down, table = pl.pallas_call(
        finish,
        out_shape=(
            jax.ShapeDtypeStruct((72, 2, C), BF),
            jax.ShapeDtypeStruct((72, 2, C), BF),
            jax.ShapeDtypeStruct((18, 2, C), F32),
            jax.ShapeDtypeStruct((6, 2, C), F32),
            jax.ShapeDtypeStruct((2, 24, C), F32),
            jax.ShapeDtypeStruct((6, 2, 768), F32),
            jax.ShapeDtypeStruct((12, 1, POS), F32),
        ),
        in_specs=[vmem] * 4,
        out_specs=[vmem] * 7,
        compiler_params=pltpu.CompilerParams(vmem_limit_bytes=60 * 1024 * 1024),
    )(*results)

    def field(value):
        return value.reshape(6, 12, 2, C).transpose(2, 0, 1, 3)

    return (
        field(mixed),
        field(grad_tokens),
        qkv.transpose(1, 2, 0),
        proj.transpose(1, 2, 0),
        up.transpose(0, 2, 1),
        down.transpose(1, 2, 0),
        table.reshape(2, 1, 1, 6, POS),
    )


def solution(mesh):
    field = P(None, "lat", "lon", None)
    table = P(None, None, "lat", None, None)
    in_specs = (field, field, P(), P(), P(), P(), P(), table, P(), P("lat"))
    columns = P(None, None, "lon")
    out_specs = (field, field, columns, columns, columns, columns, table)
    return jax.shard_map(per_device, mesh=mesh, in_specs=in_specs, out_specs=out_specs, check_vma=False)
```

time: 728 us -> 79.1 us (0.11); the launches traced: 717 us -> 77.8 us
  other arithmetic: 247 us -> 0 us
  waiting for transfers between devices: 227 us -> 0 us
  local copies, waits for them, and re-layouts: 140 us -> 0 us
  Pallas kernels: 0 us -> 77.2 us
  blocking collectives: 40.5 us -> 0 us
  matrix products: 30.5 us -> 0 us
  between operations: 17.6 us -> 0.64 us
  starting transfers between devices: 15.1 us -> 0 us
    scatter-add x2 -> x0, other arithmetic: 226 us -> none  [fold_bias(): return empty.at[:, :, :, rel_index.reshape(-1)].add(flat_grad)]
    unnamed x2 -> x0, waiting for transfers between devices: 217 us -> none
    gather x5 -> x0, local copies, waits for them, and re-layouts: 102 us -> none  [the longest x4 101 us: expand_bias(): return jnp.take(table_part, rel_index, axis=3)]
    pallas_call x0 -> x2, Pallas kernels: none -> 77.2 us  [the longest x1 75.3 us: per_device(): pl.pallas_call(functools.partial(kernel, n_lat, n_lon), out_shape=(jax.Sh...]
    psum x1 -> x0, blocking collectives: 40.5 us -> none  [per_device(): lax.psum(stacked[2].astype(jnp.bfloat16), 'lat').astype(jnp.float32)]
    dot_general x36 -> x0, matrix products: 30.5 us -> none  [the longest x8 8.55 us: matmul(): return jnp.dot(left, right, preferred_element_type=jnp.float32)]
    ppermute x8 -> x0, starting transfers between devices: 15.1 us -> none  [passed_along(): return lax.ppermute(value, axis, pairs)]
    reshape x5 -> x0, local copies, waits for them, and re-layouts: 13.8 us -> none  [the longest x4 13.6 us: fold_bias(): flat_grad = grad_bias.reshape(lead_shape + (-1,))]
  transfers between devices with their start and end apart: 9 -> 0, of which waited for: 5 -> 0; matrix products, arithmetic and copies ran while one was open for 26% -> 0% of each run, Pallas kernels for 0% -> 0%
where the time goes in v1:
time: 79.1 us; the launch traced here: 77.8 us
  Pallas kernels  77.2 us (98%)
    pallas_call x1, Pallas kernels, per_device(): pl.pallas_call(functools.partial(kernel, n_lat, n_lon), out_shape=(jax.Sh...  75.3 us
    pallas_call x1, Pallas kernels, per_device(): pl.pallas_call(finish, out_shape=(jax.ShapeDtypeStruct((72, 2, C), BF), j...  1.88 us

profile of v1, /device:TPU:8, one launch (start us, length us, event | category | flops | bytes accessed | tf_op | source)
XLA Modules:
  0.0 77.8 jit_solution(7123526123737356519)
XLA Ops:
  0.6 75.3 %shard_map.162 = (bf16[72,2,192]{2,1,0:T(2,128)(2,1)}, bf16[72,2,192]{2,1,0:T(2,128)(2,1)}, bf16[2,8,16,128]{3,2,1,0:T(8,128)(2,1)}, bf16[2,2,8,16,128]{4,3,2,1,0:T(8,128)(2,1)}) custom-call(s32[144,144]{1,0:T(8,128)} %rel_hbm.1, f32[12,1,3312]{2,1,0:T(1,128)} %bitcast.22, s32[16,768]{1,0:T(8,128)} %constant.2.clone.const_hbm, bf16[72,2,192]{2,1,0:T(2,128)(2,1)} %bitcast.23, ...), custom_call_target="tpu_custom_call" | custom-call | tf_op jit(solution)/shard_map/pallas_call | solution.py:554
  75.9 1.9 %shard_map.163 = (bf16[72,2,192]{2,1,0:T(2,128)(2,1)}, bf16[72,2,192]{2,1,0:T(2,128)(2,1)}, f32[18,2,192]{2,1,0:T(2,128)}, f32[6,2,192]{2,1,0:T(2,128)}, f32[2,2...) custom-call(bf16[72,2,192]{2,1,0:T(2,128)(2,1)} %get-tuple-element.18.mixed_in, ...), custom_call_target="tpu_custom_call" | custom-call | tf_op jit(solution)/shard_map/pallas_call | solution.py:577

commit v2 on v1

--- a/solution.py
+++ b/solution.py
@@ -40,13 +40,20 @@
     rows[5, high + other] = tok
     rows[6, high + other] = place
     rows[10, place] = high + own
+    return rows
+
+
+def permutations():
+    qkv = np.zeros((3 * C, 768), np.float32)
+    proj = np.zeros((C, 768), np.float32)
+    down = np.zeros((C, 256), np.float32)
     for piece in range(32):
         for i in range(18):
-            rows[7, 24 * piece + i] = 18 * piece + i
+            qkv[18 * piece + i, 24 * piece + i] = 1
         for i in range(6):
-            rows[8, 24 * piece + 18 + i] = 6 * piece + i
-            rows[9, 8 * piece + i] = 6 * piece + i
-    return rows
+            proj[6 * piece + i, 24 * piece + 18 + i] = 1
+            down[6 * piece + i, 8 * piece + i] = 1
+    return tuple(jnp.asarray(matrix, BF) for matrix in (qkv, proj, down))
 
 
 def dot(a, b):
@@ -75,9 +82,9 @@
 
 def kernel(
     n_lat, n_lon,
-    rel_hbm, table_hbm, const_hbm, tok_hbm, gmix_hbm, wqkv_hbm, wproj_hbm, gains_hbm, wup_hbm, wdown_hbm, ids_ref,
+    rel_hbm, table_hbm, const_hbm, tok_hbm, gmix_hbm, wqkv_hbm, wproj_hbm, gains_hbm, wup_hbm, wdown_hbm, pq_hbm, pp_hbm, pd_hbm, ids_ref,
     mixed_ref, gtok_ref, wg_ref, tgrad_ref,
-    rel_ref, table_ref, const_ref, tok_ref, gmix_ref, wqkv_ref, wproj_ref, gains_ref, wup_ref, wdown_ref, load_sem,
+    rel_ref, table_ref, const_ref, tok_ref, gmix_ref, wqkv_ref, wproj_ref, gains_ref, wup_ref, wdown_ref, pq_ref, pp_ref, pd_ref, load_sem,
     x_ref, qkv_ref, qm_ref, s_ref, p_ref, att_ref, u1_ref, i1_ref, mid_ref, gp_ref, hid_ref, u2_ref, i2_ref,
     gup_ref, gam_ref, ds_ref, idx_ref, low_ref, oht_ref, tabf_ref, tab_ref, bias_ref, btail_ref, pk_ref, gall_ref, acc_ref,
     l_ref, r_ref, o1_ref, o3_ref,
@@ -91,6 +98,7 @@
         for k, (src, dst) in enumerate([
             (rel_hbm, rel_ref), (table_hbm, table_ref), (const_hbm, const_ref), (tok_hbm, tok_ref), (gmix_hbm, gmix_ref),
             (wqkv_hbm, wqkv_ref), (wproj_hbm, wproj_ref), (gains_hbm, gains_ref), (wup_hbm, wup_ref), (wdown_hbm, wdown_ref),
+            (pq_hbm, pq_ref), (pp_hbm, pp_ref), (pd_hbm, pd_ref),
         ])
     ]
     for load in loads:
@@ -158,9 +166,11 @@
             rolled = pltpu.roll(value, (128 - 16 * j) % 128, 1)
             btail_ref[k, pl.ds(j, 24, stride=8), :] = rolled
 
-    def gather_biases():
+    def gather_bias(b):
         place = lax.broadcasted_iota(jnp.int32, (256, 128), 0).astype(BF)
+        place_t = lax.broadcasted_iota(jnp.int32, (128, 256), 1).astype(BF)
         one, zero = jnp.ones((256, 128), BF), jnp.zeros((256, 128), BF)
+        one_t, zero_t = jnp.ones((128, 256), BF), jnp.zeros((128, 256), BF)
 
         def step(i, carry):
             index = idx_ref[pl.ds(pl.multiple_of(i * 8, 8), 8), :]
@@ -169,39 +179,28 @@
             for r in range(8):
                 row = jnp.broadcast_to(low[r : r + 1, :], (16, 128)).astype(BF)
                 picks.append(jnp.where(place == jnp.concatenate([row] * 16, axis=0), one, zero))
-            rows = dot(tab_ref[...], jnp.concatenate(picks, axis=1))
+            rows = dot(tab_ref[b], jnp.concatenate(picks, axis=1))
             for r in range(8):
-                high_row = jnp.broadcast_to(high[r : r + 1, :], (16, 128))
-                found = jnp.zeros((16, 128), F32)
+                high_row = jnp.broadcast_to(high[r : r + 1, :], (8, 128))
+                found = jnp.zeros((8, 128), F32)
                 for part in range(13):
-                    coarse = rows[16 * part : 16 * part + 16, 128 * r : 128 * r + 128]
-                    fine = rows[208 + 16 * part : 224 + 16 * part, 128 * r : 128 * r + 128]
+                    coarse = rows[8 * part : 8 * part + 8, 128 * r : 128 * r + 128]
+                    fine = rows[104 + 8 * part : 112 + 8 * part, 128 * r : 128 * r + 128]
                     found = jnp.where(high_row == part, coarse + fine, found)
-                bias_ref[pl.ds(pl.multiple_of(i * 128 + r * 16, 16), 16), :] = found
+                bias_ref[b, pl.ds(pl.multiple_of(i * 64 + r * 8, 8), 8), :] = found
+            if b == 0:
+                block = low_ref[i]
+                for r in range(8):
+                    span = pl.ds(pl.multiple_of(i * 1024 + r * 128, 128), 128)
+                    column = jnp.broadcast_to(block[:, r : r + 1], (128, 128)).astype(BF)
+                    oht_ref[span, :] = jnp.where(place_t == jnp.concatenate([column] * 2, axis=1), one_t, zero_t)
             return carry
 
         lax.fori_loop(0, ROWS // 8, step, 0)
-        for b in range(2):
-            for h in range(HEADS):
-                unpack_tail(bias_ref[pl.ds(16 * TAIL + 8 * b + h, 24, stride=16), :], 6 * b + h)
-
-    def expand_index():
-        place = lax.broadcasted_iota(jnp.int32, (128, 256), 1).astype(BF)
-        one, zero = jnp.ones((128, 256), BF), jnp.zeros((128, 256), BF)
-
-        def step(i, carry):
-            block = low_ref[i]
-            for r in range(8):
-                span = pl.ds(pl.multiple_of(i * 1024 + r * 128, 128), 128)
-                column = jnp.broadcast_to(block[:, r : r + 1], (128, 128)).astype(BF)
-                oht_ref[span, :] = jnp.where(place == jnp.concatenate([column] * 2, axis=1), one, zero)
-            return carry
-
-        lax.fori_loop(0, ROWS // 8, step, 0)
-
-    def fold_tables():
-        acc_ref[...] = jnp.zeros_like(acc_ref)
-
+        for h in range(HEADS):
+            unpack_tail(bias_ref[b, pl.ds(8 * TAIL + h, 24, stride=8), :], 6 * b + h)
+
+    def fold_tables(start, stop):
         def step(i, carry):
             high = idx_ref[pl.ds(pl.multiple_of(i * 8, 8), 8), :] >> 8
             left = [[] for _ in range(26)]
@@ -215,7 +214,7 @@
             acc_ref[...] += dot(left, oht_ref[pl.ds(pl.multiple_of(i * 1024, 1024), 1024), :])
             return carry
 
-        lax.fori_loop(0, ROWS // 8, step, 0)
+        lax.fori_loop(start, stop, step, 0)
 
     def region_codes(place):
         code = jnp.zeros_like(place)
@@ -237,7 +236,7 @@
             allowed = codes_s == codes_t
         for h in range(HEADS):
             span = pl.ds(TOK * h, TOK)
-            main = bias_ref[pl.ds(8 * b + h, TOK, stride=16), :]
+            main = bias_ref[b, pl.ds(h, TOK, stride=8), :]
             bias = jnp.concatenate([main, btail_ref[6 * b + h, 0:TOK, 0:16]], axis=1)
             scores = s_ref[span, :] * SCALE + bias
             if b == 1:
@@ -264,7 +263,7 @@
         u2_ref[b], i2_ref[b] = unit, inverse
         return (middle.astype(F32) + unit * gains_ref[b, 1:2, :]).astype(BF)
 
-    def backward(b, grad, between):
+    def backward(b, grad, between=lambda: None):
         grad = grad.astype(F32)
         grad_down = norm_back(grad * gains_ref[b, 1:2, :], u2_ref[b], i2_ref[b]).astype(BF)
         for part in range(3):
@@ -279,7 +278,6 @@
             gam_ref[TOK * h : TOK * h + TOK, :] = of_head(grad_att, h)
         q, k, v = (qkv_ref[b, :, C * i : C * i + C] for i in range(3))
         s_ref[...] = dot_nt(gam_ref[...], v)
-        between()
         for h in range(HEADS):
             span = pl.ds(TOK * h, TOK)
             probs = p_ref[b, span, :].astype(F32)
@@ -288,7 +286,6 @@
             ds_ref[span, :] = grad_scores.astype(BF)
             gall_ref[b, pl.ds(h, TOK, stride=8), :] = grad_scores[:, 0:128]
             gall_ref[b, pl.ds(8 * TAIL + h, 24, stride=8), :] = pack_tail(grad_scores[:, 128:TOK], h)
-        between()
         grad_q = jnp.zeros((TOK, C), F32)
         for h in range(HEADS):
             grad_q = jnp.where(head_lanes[h], dot(ds_ref[TOK * h : TOK * h + TOK, :], k), grad_q)
@@ -299,8 +296,8 @@
         return grad_in, grad_down, grad_pre, grad_qkv
 
     def weight_grads(b, grad_down, grad_pre, grad_qkv):
-        l_ref[0:TOK, :] = moved(grad_qkv, onehot(3 * C, 768, 7))
-        l_ref[TOK : 2 * TOK, :] = moved(grad_pre, onehot(C, 768, 8))
+        l_ref[0:TOK, :] = moved(grad_qkv, pq_ref[...])
+        l_ref[TOK : 2 * TOK, :] = moved(grad_pre, pp_ref[...])
         l_ref[2 * TOK : 3 * TOK, :] = gup_ref[b]
         tokens, middle = x_ref[b], mid_ref[b]
         r_ref[0:TOK, 0:128] = tokens[:, 0:128]
@@ -310,7 +307,7 @@
         r_ref[2 * TOK : 3 * TOK, 128:256] = middle[:, 0:128]
         r_ref[2 * TOK : 3 * TOK, 320:384] = middle[:, 128:C]
         o1_ref[...] = dot_tn(l_ref[...], r_ref[...])
-        o3_ref[...] = dot_tn(moved(grad_down, onehot(C, 256, 9)), hid_ref[b])
+        o3_ref[...] = dot_tn(moved(grad_down, pd_ref[...]), hid_ref[b])
         rows = 128 // n_lat
         for piece in range(32):
             units = [o1_ref[24 * piece + 8 * i : 24 * piece + 8 * i + 8, 128 * m : 128 * m + 128] for m in range(3) for i in range(3)]
@@ -446,14 +443,12 @@
     for b in range(2):
         for part in range(13):
             width = min(256, POS - 256 * part)
-            tabf_ref[16 * part + 8 * b : 16 * part + 8 * b + 6, 0:width] = table_ref[
-                6 * b : 6 * b + 6, 0, 256 * part : 256 * part + width
-            ]
-    table = tabf_ref[...]
-    coarse = table.astype(BF)
-    tab_ref[0:208, :] = coarse
-    tab_ref[208:416, :] = (table - coarse.astype(F32)).astype(BF)
-    gather_biases()
+            tabf_ref[b, 8 * part : 8 * part + 6, 0:width] = table_ref[6 * b : 6 * b + 6, 0, 256 * part : 256 * part + width]
+        table = tabf_ref[b]
+        coarse = table.astype(BF)
+        tab_ref[b, 0:104, :] = coarse
+        tab_ref[b, 104:208, :] = (table - coarse.astype(F32)).astype(BF)
+    gather_bias(0)
     for load in loads[2:]:
         load.wait()
     x_ref[0] = moved(onehot(TOK, TOK, 0), tok_ref[...].reshape(TOK, C))
@@ -464,7 +459,8 @@
     pl.semaphore_wait(barrier, len(greeted))
     copies_x = send_quarters(1, ahead)
     copies_g = send_quarters(0, ahead)
-    expand_index()
+    gather_bias(1)
+    acc_ref[...] = jnp.zeros_like(acc_ref)
     arrive(copies_x)
     arrive(copies_g)
     come = onehot(TOK, 192, 3)
@@ -473,7 +469,7 @@
 
     second = forward(1)
     hs_ref[2] = moved(onehot(192, TOK, 4), second).reshape(4, 48, C)
-    grad_second, *rest = backward(1, grad_shifted, lambda: None)
+    grad_second, *rest = backward(1, grad_shifted)
     hs_ref[3] = moved(onehot(192, TOK, 4), grad_second).reshape(4, 48, C)
     copies_s = send_quarters(3, back)
     copies_m = send_quarters(2, back)
@@ -486,18 +482,25 @@
     grad_in, *rest = backward(0, grad_first, sum_two.next)
     weight_grads(0, *rest)
     sum_one = Sum(0)
+    sum_table = TableSum()
     sum_one.next()
+    sum_two.next()
+    fold_tables(0, 9)
     sum_one.next()
-    fold_tables()
-    sum_table = TableSum()
+    fold_tables(9, ROWS // 8)
     sum_table.next()
+    sum_two.next()
     arrive(copies_m)
     mixed_ref[...] = moved(onehot(TOK, 192, 6), hr_ref[2].reshape(192, C)).reshape(72, 2, C)
     gtok_ref[...] = moved(onehot(TOK, TOK, 1), grad_in).reshape(72, 2, C)
-    for _ in range(5):
-        sum_one.next()
-        sum_table.next()
-        sum_two.next()
+    sum_table.next()
+    sum_two.next()
+    sum_table.next()
+    sum_one.next()
+    sum_table.next()
+    sum_one.next()
+    sum_table.next()
+    sum_one.next()
     for copy in sent:
         copy.wait_send()
 
@@ -534,13 +537,14 @@
     scratch = [
         buf(TOK, TOK, dtype=jnp.int32), buf(12, 1, POS, dtype=F32), buf(16, 768, dtype=jnp.int32),
         buf(72, 2, C), buf(72, 2, C), buf(2, C, 3 * C), buf(2, C, C), buf(2, 2, C, dtype=F32), buf(2, C, 768), buf(2, C, 768),
-        pltpu.SemaphoreType.DMA((10,)),
+        buf(3 * C, 768), buf(C, 768), buf(C, 256),
+        pltpu.SemaphoreType.DMA((13,)),
         buf(2, TOK, C), buf(2, TOK, 3 * C), buf(2, 6 * TOK, C), buf(6 * TOK, TOK, dtype=F32),
         buf(2, 6 * TOK, TOK), buf(2, TOK, C), buf(2, TOK, C, dtype=F32), buf(2, TOK, 1, dtype=F32), buf(2, TOK, C),
         buf(2, TOK, 768, dtype=F32), buf(2, TOK, 768), buf(2, TOK, C, dtype=F32), buf(2, TOK, 1, dtype=F32),
         buf(2, TOK, 768), buf(6 * TOK, C), buf(6 * TOK, TOK),
-        buf(ROWS, 128, dtype=jnp.int32), buf(ROWS // 8, 128, 8, dtype=F32), buf(128 * ROWS, 256), buf(208, 256, dtype=F32),
-        buf(416, 256), buf(16 * ROWS, 128, dtype=F32), buf(12, 192, 128, dtype=F32), buf(6, 192, 128, dtype=F32),
+        buf(ROWS, 128, dtype=jnp.int32), buf(ROWS // 8, 128, 8, dtype=F32), buf(128 * ROWS, 256), buf(2, 104, 256, dtype=F32),
+        buf(2, 208, 256), buf(2, 8 * ROWS, 128, dtype=F32), buf(12, 192, 128, dtype=F32), buf(6, 192, 128, dtype=F32),
         buf(2, 8 * ROWS, 128, dtype=F32), buf(208, 256, dtype=F32),
         buf(3 * TOK, 768), buf(3 * TOK, 384), buf(768, 384, dtype=F32), buf(256, 768, dtype=F32),
         buf(4, 4, 48, C), buf(4, 4, 48, C),
@@ -559,7 +563,7 @@
             jax.ShapeDtypeStruct((2, n_lat, rows, 128), BF),
             jax.ShapeDtypeStruct((2, 2, 8, 16, 128), BF),
         ),
-        in_specs=[pl.BlockSpec(memory_space=pltpu.HBM)] * 10 + [smem],
+        in_specs=[pl.BlockSpec(memory_space=pltpu.HBM)] * 13 + [smem],
         out_specs=[vmem] * 4,
         scratch_shapes=scratch,
         compiler_params=pltpu.CompilerParams(
@@ -572,6 +576,7 @@
         tokens.transpose(1, 2, 0, 3).reshape(72, 2, C),
         grad_mixed.transpose(1, 2, 0, 3).reshape(72, 2, C),
         w_qkv, w_proj, gains, w_up, w_down.transpose(0, 2, 1),
+        *permutations(),
         mask_ids,
     )
     mixed, grad_tokens, qkv, proj, up, down, table = pl.pallas_call(

time: 79.1 us -> 73.2 us (0.925); the launches traced: 77.8 us -> 73.1 us
  Pallas kernels: 77.2 us -> 72.5 us
    pallas_call x1, Pallas kernels: 75.3 us -> 70.6 us  [per_device(): pl.pallas_call(functools.partial(kernel, n_lat, n_lon), out_shape=(jax.Sh...]
where the time goes in v2:
time: 73.2 us; the launch traced here: 73.1 us
  Pallas kernels  72.5 us (99%)
    pallas_call x1, Pallas kernels, per_device(): pl.pallas_call(functools.partial(kernel, n_lat, n_lon), out_shape=(jax.Sh...  70.6 us
    pallas_call x1, Pallas kernels, per_device(): pl.pallas_call(finish, out_shape=(jax.ShapeDtypeStruct((72, 2, C), BF), j...  1.88 us

profile of v2, /device:TPU:8, one launch (start us, length us, event | category | flops | bytes accessed | tf_op | source)
XLA Modules:
  0.0 73.1 jit_solution(17850265908519871340)
XLA Ops:
  0.6 70.6 %shard_map.189 = (bf16[72,2,192]{2,1,0:T(2,128)(2,1)}, bf16[72,2,192]{2,1,0:T(2,128)(2,1)}, bf16[2,8,16,128]{3,2,1,0:T(8,128)(2,1)}, bf16[2,2,8,16,128]{4,3,2,1,0:T(8,128)(2,1)}) custom-call(s32[144,144]{1,0:T(8,128)} %rel_hbm.1, f32[12,1,3312]{2,1,0:T(1,128)} %bitcast.22, s32[16,768]{1,0:T(8,128)} %constant.8.clone.const_hbm, bf16[72,2,192]{2,1,0:T(2,128)(2,1)} %bitcast.23, ...), custom_call_target="tpu_custom_call" | custom-call | tf_op jit(solution)/shard_map/pallas_call | solution.py:558
  71.2 1.9 %shard_map.190 = (bf16[72,2,192]{2,1,0:T(2,128)(2,1)}, bf16[72,2,192]{2,1,0:T(2,128)(2,1)}, f32[18,2,192]{2,1,0:T(2,128)}, f32[6,2,192]{2,1,0:T(2,128)}, f32[2,2...) custom-call(bf16[72,2,192]{2,1,0:T(2,128)(2,1)} %get-tuple-element.18.mixed_in, ...), custom_call_target="tpu_custom_call" | custom-call | tf_op jit(solution)/shard_map/pallas_call | solution.py:582

commit v3 on v2

--- a/solution.py
+++ b/solution.py
@@ -18,9 +18,9 @@
 BF = jnp.bfloat16
 F32 = jnp.float32
 MESH = pl.DeviceIdType.MESH
-ROWS = 168
+ROWS = 192
 TAIL = 144
-N_SEMS = 92
+N_SEMS = 94
 
 
 def index_rows():
@@ -85,8 +85,8 @@
     rel_hbm, table_hbm, const_hbm, tok_hbm, gmix_hbm, wqkv_hbm, wproj_hbm, gains_hbm, wup_hbm, wdown_hbm, pq_hbm, pp_hbm, pd_hbm, ids_ref,
     mixed_ref, gtok_ref, wg_ref, tgrad_ref,
     rel_ref, table_ref, const_ref, tok_ref, gmix_ref, wqkv_ref, wproj_ref, gains_ref, wup_ref, wdown_ref, pq_ref, pp_ref, pd_ref, load_sem,
-    x_ref, qkv_ref, qm_ref, s_ref, p_ref, att_ref, u1_ref, i1_ref, mid_ref, gp_ref, hid_ref, u2_ref, i2_ref,
-    gup_ref, gam_ref, ds_ref, idx_ref, low_ref, oht_ref, tabf_ref, tab_ref, bias_ref, btail_ref, pk_ref, gall_ref, acc_ref,
+    x_ref, qkv_ref, km_ref, vm_ref, s_ref, p_ref, att_ref, u1_ref, i1_ref, mid_ref, gp_ref, hid_ref, u2_ref, i2_ref,
+    gup_ref, ds_ref, idx_ref, low_ref, tabf_ref, tab_ref, bias_ref, btail_ref, pk_ref, gall_ref, gsend_ref, grecv_ref, acc_ref,
     l_ref, r_ref, o1_ref, o3_ref,
     hs_ref, hr_ref,
     sb_ref, rc_ref, wa_ref, rx_ref, wc_ref, rz_ref, wd_ref, wl_ref,
@@ -168,50 +168,66 @@
 
     def gather_bias(b):
         place = lax.broadcasted_iota(jnp.int32, (256, 128), 0).astype(BF)
-        place_t = lax.broadcasted_iota(jnp.int32, (128, 256), 1).astype(BF)
         one, zero = jnp.ones((256, 128), BF), jnp.zeros((256, 128), BF)
-        one_t, zero_t = jnp.ones((128, 256), BF), jnp.zeros((128, 256), BF)
 
         def step(i, carry):
-            index = idx_ref[pl.ds(pl.multiple_of(i * 8, 8), 8), :]
-            low, high = (index & 255).astype(F32), index >> 8
-            picks = []
-            for r in range(8):
-                row = jnp.broadcast_to(low[r : r + 1, :], (16, 128)).astype(BF)
-                picks.append(jnp.where(place == jnp.concatenate([row] * 16, axis=0), one, zero))
-            rows = dot(tab_ref[b], jnp.concatenate(picks, axis=1))
-            for r in range(8):
-                high_row = jnp.broadcast_to(high[r : r + 1, :], (8, 128))
-                found = jnp.zeros((8, 128), F32)
-                for part in range(13):
-                    coarse = rows[8 * part : 8 * part + 8, 128 * r : 128 * r + 128]
-                    fine = rows[104 + 8 * part : 112 + 8 * part, 128 * r : 128 * r + 128]
-                    found = jnp.where(high_row == part, coarse + fine, found)
-                bias_ref[b, pl.ds(pl.multiple_of(i * 64 + r * 8, 8), 8), :] = found
-            if b == 0:
-                block = low_ref[i]
+            for m in range(3):
+                group = i * 3 + m
+                index = idx_ref[pl.ds(pl.multiple_of(group * 8, 8), 8), :]
+                low, high = (index & 255).astype(F32), index >> 8
+                picks = []
                 for r in range(8):
-                    span = pl.ds(pl.multiple_of(i * 1024 + r * 128, 128), 128)
+                    row = jnp.broadcast_to(low[r : r + 1, :], (16, 128)).astype(BF)
+                    picks.append(jnp.where(place == jnp.concatenate([row] * 16, axis=0), one, zero))
+                rows = dot(tab_ref[b], jnp.concatenate(picks, axis=1))
+                for r in range(8):
+                    high_row = jnp.broadcast_to(high[r : r + 1, :], (8, 128))
+                    found = jnp.zeros((8, 128), F32)
+                    for part in range(13):
+                        coarse = rows[8 * part : 8 * part + 8, 128 * r : 128 * r + 128]
+                        fine = rows[104 + 8 * part : 112 + 8 * part, 128 * r : 128 * r + 128]
+                        found = jnp.where(high_row == part, coarse + fine, found)
+                    bias_ref[pl.ds(pl.multiple_of(group * 64 + r * 8, 8), 8), :] = found
+            return carry
+
+        lax.fori_loop(0, 7, step, 0)
+        for h in range(HEADS):
+            unpack_tail(bias_ref[pl.ds(8 * TAIL + h, 24, stride=8), :], h)
+
+    half = ROWS // 2
+
+    def share_scores(b):
+        gsend_ref[b] = gall_ref[b, pl.ds((1 - co) * 8 * half, 8 * half), :].astype(BF)
+        return [push(gsend_ref.at[b], grecv_ref.at[b], (lat, lon + 1 - 2 * co))]
+
+    def add_scores(b, copies):
+        arrive(copies)
+        mine = pl.ds(co * 8 * half, 8 * half)
+        gall_ref[b, mine, :] = gall_ref[b, mine, :] + grecv_ref[b].astype(F32)
+
+    def fold_tables(start, stop):
+        place = lax.broadcasted_iota(jnp.int32, (128, 256), 1).astype(BF)
+        one, zero = jnp.ones((128, 256), BF), jnp.zeros((128, 256), BF)
+
+        def step(i, carry):
+            total = acc_ref[...]
+            for m in range(3):
+                group = co * (half // 8) + i * 3 + m
+                high = idx_ref[pl.ds(pl.multiple_of(group * 8, 8), 8), :] >> 8
+                block = low_ref[group]
+                left, right = [[] for _ in range(26)], []
+                for r in range(8):
+                    high_row = jnp.broadcast_to(high[r : r + 1, :], (8, 128))
+                    hits = [high_row == part for part in range(13)]
+                    for b in range(2):
+                        grads = gall_ref[b, pl.ds(pl.multiple_of(group * 64 + r * 8, 8), 8), :]
+                        for part in range(13):
+                            left[13 * b + part].append(jnp.where(hits[part], grads, 0.0))
                     column = jnp.broadcast_to(block[:, r : r + 1], (128, 128)).astype(BF)
-                    oht_ref[span, :] = jnp.where(place_t == jnp.concatenate([column] * 2, axis=1), one_t, zero_t)
-            return carry
-
-        lax.fori_loop(0, ROWS // 8, step, 0)
-        for h in range(HEADS):
-            unpack_tail(bias_ref[b, pl.ds(8 * TAIL + h, 24, stride=8), :], 6 * b + h)
-
-    def fold_tables(start, stop):
-        def step(i, carry):
-            high = idx_ref[pl.ds(pl.multiple_of(i * 8, 8), 8), :] >> 8
-            left = [[] for _ in range(26)]
-            for r in range(8):
-                high_row = jnp.broadcast_to(high[r : r + 1, :], (8, 128))
-                for b in range(2):
-                    grads = gall_ref[b, pl.ds(pl.multiple_of(i * 64 + r * 8, 8), 8), :]
-                    for part in range(13):
-                        left[13 * b + part].append(jnp.where(high_row == part, grads, 0.0))
-            left = jnp.concatenate([jnp.concatenate(rows, axis=1) for rows in left], axis=0).astype(BF)
-            acc_ref[...] += dot(left, oht_ref[pl.ds(pl.multiple_of(i * 1024, 1024), 1024), :])
+                    right.append(jnp.where(place == jnp.concatenate([column] * 2, axis=1), one, zero))
+                left = jnp.concatenate([jnp.concatenate(rows, axis=1) for rows in left], axis=0).astype(BF)
+                total = total + dot(left, jnp.concatenate(right, axis=0))
+            acc_ref[...] = total
             return carry
 
         lax.fori_loop(start, stop, step, 0)
@@ -228,26 +244,23 @@
         qkv_ref[b] = dot(tokens, wqkv_ref[b]).astype(BF)
         q, k, v = (qkv_ref[b, :, C * i : C * i + C] for i in range(3))
         for h in range(HEADS):
-            qm_ref[b, TOK * h : TOK * h + TOK, :] = of_head(q, h)
-        s_ref[...] = dot_nt(qm_ref[b], k)
+            km_ref[b, TOK * h : TOK * h + TOK, :] = of_head(k, h)
+            vm_ref[b, TOK * h : TOK * h + TOK, :] = of_head(v, h)
+        s_ref[...] = dot_nt(km_ref[b], q)
         if b == 1:
-            codes_s = region_codes(lax.broadcasted_iota(jnp.int32, (TOK, 1), 0))
-            codes_t = region_codes(lax.broadcasted_iota(jnp.int32, (1, TOK), 1))
+            codes_t = region_codes(lax.broadcasted_iota(jnp.int32, (TOK, 1), 0))
+            codes_s = region_codes(lax.broadcasted_iota(jnp.int32, (1, TOK), 1))
             allowed = codes_s == codes_t
         for h in range(HEADS):
             span = pl.ds(TOK * h, TOK)
-            main = bias_ref[b, pl.ds(h, TOK, stride=8), :]
-            bias = jnp.concatenate([main, btail_ref[6 * b + h, 0:TOK, 0:16]], axis=1)
+            bias = jnp.concatenate([bias_ref[pl.ds(h, TOK, stride=8), :], btail_ref[h, 0:TOK, 0:16]], axis=1)
             scores = s_ref[span, :] * SCALE + bias
             if b == 1:
                 scores = jnp.where(allowed, scores, NEGATIVE)
-            powers = jnp.exp(scores - jnp.max(scores, axis=-1, keepdims=True))
-            probs = powers * (1.0 / jnp.sum(powers, axis=-1, keepdims=True))
+            powers = jnp.exp(scores - jnp.max(scores, axis=0, keepdims=True))
+            probs = powers * (1.0 / jnp.sum(powers, axis=0, keepdims=True))
             p_ref[b, span, :] = probs.astype(BF)
-        attended = jnp.zeros((TOK, C), F32)
-        for h in range(HEADS):
-            attended = jnp.where(head_lanes[h], dot(p_ref[b, TOK * h : TOK * h + TOK, :], v), attended)
-        attended = attended.astype(BF)
+        attended = dot_tn(p_ref[b], vm_ref[b]).astype(BF)
         att_ref[b] = attended
         unit, inverse = norm_parts(dot(attended, wproj_ref[b]))
         u1_ref[b], i1_ref[b] = unit, inverse
@@ -274,23 +287,22 @@
         between()
         grad_pre = norm_back(grad_middle * gains_ref[b, 0:1, :], u1_ref[b], i1_ref[b]).astype(BF)
         grad_att = dot_nt(grad_pre, wproj_ref[b]).astype(BF)
-        for h in range(HEADS):
-            gam_ref[TOK * h : TOK * h + TOK, :] = of_head(grad_att, h)
-        q, k, v = (qkv_ref[b, :, C * i : C * i + C] for i in range(3))
-        s_ref[...] = dot_nt(gam_ref[...], v)
+        q = qkv_ref[b, :, 0:C]
+        s_ref[...] = dot_nt(vm_ref[b], grad_att)
         for h in range(HEADS):
             span = pl.ds(TOK * h, TOK)
             probs = p_ref[b, span, :].astype(F32)
             grad_probs = s_ref[span, :]
-            grad_scores = probs * (grad_probs - jnp.sum(grad_probs * probs, axis=-1, keepdims=True))
+            grad_scores = probs * (grad_probs - jnp.sum(grad_probs * probs, axis=0, keepdims=True))
             ds_ref[span, :] = grad_scores.astype(BF)
             gall_ref[b, pl.ds(h, TOK, stride=8), :] = grad_scores[:, 0:128]
             gall_ref[b, pl.ds(8 * TAIL + h, 24, stride=8), :] = pack_tail(grad_scores[:, 128:TOK], h)
-        grad_q = jnp.zeros((TOK, C), F32)
+        grad_q = dot_tn(ds_ref[...], km_ref[b])
+        grad_k, grad_v = jnp.zeros((TOK, C), F32), jnp.zeros((TOK, C), F32)
         for h in range(HEADS):
-            grad_q = jnp.where(head_lanes[h], dot(ds_ref[TOK * h : TOK * h + TOK, :], k), grad_q)
-        grad_k = dot_tn(ds_ref[...], qm_ref[b])
-        grad_v = dot_tn(p_ref[b], gam_ref[...])
+            span = pl.ds(TOK * h, TOK)
+            grad_k = jnp.where(head_lanes[h], dot(ds_ref[span, :], q), grad_k)
+            grad_v = jnp.where(head_lanes[h], dot(p_ref[b, span, :], grad_att), grad_v)
         grad_qkv = jnp.concatenate([grad_q * SCALE, grad_k * SCALE, grad_v], axis=1).astype(BF)
         grad_in = (grad_middle + dot_nt(grad_qkv, wqkv_ref[b])).astype(BF)
         return grad_in, grad_down, grad_pre, grad_qkv
@@ -432,8 +444,9 @@
     gall_ref[...] = jnp.zeros_like(gall_ref)
     r_ref[...] = jnp.zeros_like(r_ref)
     loads[0].wait()
-    idx_ref[0:TOK, :] = rel_ref[:, 0:128]
-    idx_ref[TAIL:ROWS, :] = pack_tail(rel_ref[:, 128:TOK].astype(F32), 0).astype(jnp.int32)
+    relative = rel_ref[...].astype(F32).T
+    idx_ref[0:TOK, :] = relative[:, 0:128].astype(jnp.int32)
+    idx_ref[TAIL : TAIL + 24, :] = pack_tail(relative[:, 128:TOK], 0).astype(jnp.int32)
     idx_ref[TAIL + 18 : ROWS, :] = jnp.full((ROWS - TAIL - 18, 128), -1, jnp.int32)
     low = (idx_ref[...] & 255).astype(F32).T
     for i in range(ROWS // 8):
@@ -473,6 +486,7 @@
     hs_ref[3] = moved(onehot(192, TOK, 4), grad_second).reshape(4, 48, C)
     copies_s = send_quarters(3, back)
     copies_m = send_quarters(2, back)
+    copies_two = share_scores(1)
     weight_grads(1, *rest)
     sum_two = Sum(1)
     sum_two.next()
@@ -480,14 +494,17 @@
     arrive(copies_s)
     grad_first = moved(onehot(TOK, 192, 5), hr_ref[3].reshape(192, C))
     grad_in, *rest = backward(0, grad_first, sum_two.next)
+    copies_one = share_scores(0)
     weight_grads(0, *rest)
     sum_one = Sum(0)
     sum_table = TableSum()
     sum_one.next()
     sum_two.next()
-    fold_tables(0, 9)
+    add_scores(1, copies_two)
+    add_scores(0, copies_one)
+    fold_tables(0, 2)
     sum_one.next()
-    fold_tables(9, ROWS // 8)
+    fold_tables(2, 4)
     sum_table.next()
     sum_two.next()
     arrive(copies_m)
@@ -539,13 +556,13 @@
         buf(72, 2, C), buf(72, 2, C), buf(2, C, 3 * C), buf(2, C, C), buf(2, 2, C, dtype=F32), buf(2, C, 768), buf(2, C, 768),
         buf(3 * C, 768), buf(C, 768), buf(C, 256),
         pltpu.SemaphoreType.DMA((13,)),
-        buf(2, TOK, C), buf(2, TOK, 3 * C), buf(2, 6 * TOK, C), buf(6 * TOK, TOK, dtype=F32),
+        buf(2, TOK, C), buf(2, TOK, 3 * C), buf(2, 6 * TOK, C), buf(2, 6 * TOK, C), buf(6 * TOK, TOK, dtype=F32),
         buf(2, 6 * TOK, TOK), buf(2, TOK, C), buf(2, TOK, C, dtype=F32), buf(2, TOK, 1, dtype=F32), buf(2, TOK, C),
         buf(2, TOK, 768, dtype=F32), buf(2, TOK, 768), buf(2, TOK, C, dtype=F32), buf(2, TOK, 1, dtype=F32),
-        buf(2, TOK, 768), buf(6 * TOK, C), buf(6 * TOK, TOK),
-        buf(ROWS, 128, dtype=jnp.int32), buf(ROWS // 8, 128, 8, dtype=F32), buf(128 * ROWS, 256), buf(2, 104, 256, dtype=F32),
-        buf(2, 208, 256), buf(2, 8 * ROWS, 128, dtype=F32), buf(12, 192, 128, dtype=F32), buf(6, 192, 128, dtype=F32),
-        buf(2, 8 * ROWS, 128, dtype=F32), buf(208, 256, dtype=F32),
+        buf(2, TOK, 768), buf(6 * TOK, TOK),
+        buf(ROWS, 128, dtype=jnp.int32), buf(ROWS // 8, 128, 8, dtype=F32), buf(2, 104, 256, dtype=F32), buf(2, 208, 256),
+        buf(8 * 168, 128, dtype=F32), buf(6, 192, 128, dtype=F32), buf(6, 192, 128, dtype=F32),
+        buf(2, 8 * ROWS, 128, dtype=F32), buf(2, 4 * ROWS, 128), buf(2, 4 * ROWS, 128), buf(208, 256, dtype=F32),
         buf(3 * TOK, 768), buf(3 * TOK, 384), buf(768, 384, dtype=F32), buf(256, 768, dtype=F32),
         buf(4, 4, 48, C), buf(4, 4, 48, C),
         buf(2, 2, ny, 4, nz, rows, 128), buf(2, ny, 4, nz, rows, 128), buf(2, ny, 4, nz, rows, 128),

time: 73.2 us -> 67.4 us (0.921)
  Pallas kernels: 72.5 us -> 66.7 us
    pallas_call x1, Pallas kernels: 70.6 us -> 64.8 us  [per_device(): pl.pallas_call(functools.partial(kernel, n_lat, n_lon), out_shape=(jax.Sh...]
where the time goes in v3:
time: 67.4 us; the launch traced here: 67.3 us
  Pallas kernels  66.7 us (99%)
    pallas_call x1, Pallas kernels, per_device(): pl.pallas_call(functools.partial(kernel, n_lat, n_lon), out_shape=(jax.Sh...  64.8 us
    pallas_call x1, Pallas kernels, per_device(): pl.pallas_call(finish, out_shape=(jax.ShapeDtypeStruct((72, 2, C), BF), j...  1.88 us

profile of v3, /device:TPU:8, one launch (start us, length us, event | category | flops | bytes accessed | tf_op | source)
XLA Modules:
  0.0 67.3 jit_solution(13640077515028371540)
XLA Ops:
  0.6 64.8 %shard_map.189 = (bf16[72,2,192]{2,1,0:T(2,128)(2,1)}, bf16[72,2,192]{2,1,0:T(2,128)(2,1)}, bf16[2,8,16,128]{3,2,1,0:T(8,128)(2,1)}, bf16[2,2,8,16,128]{4,3,2,1,0:T(8,128)(2,1)}) custom-call(s32[144,144]{1,0:T(8,128)} %rel_hbm.1, f32[12,1,3312]{2,1,0:T(1,128)} %bitcast.22, s32[16,768]{1,0:T(8,128)} %constant.8.clone.const_hbm, bf16[72,2,192]{2,1,0:T(2,128)(2,1)} %bitcast.23, ...), custom_call_target="tpu_custom_call" | custom-call | tf_op jit(solution)/shard_map/pallas_call | solution.py:575
  65.5 1.9 %shard_map.190 = (bf16[72,2,192]{2,1,0:T(2,128)(2,1)}, bf16[72,2,192]{2,1,0:T(2,128)(2,1)}, f32[18,2,192]{2,1,0:T(2,128)}, f32[6,2,192]{2,1,0:T(2,128)}, f32[2,2...) custom-call(bf16[72,2,192]{2,1,0:T(2,128)(2,1)} %get-tuple-element.18.mixed_in, ...), custom_call_target="tpu_custom_call" | custom-call | tf_op jit(solution)/shard_map/pallas_call | solution.py:599

commit v4 on v3

--- a/solution.py
+++ b/solution.py
@@ -20,7 +20,7 @@
 MESH = pl.DeviceIdType.MESH
 ROWS = 192
 TAIL = 144
-N_SEMS = 94
+N_SEMS = 132
 
 
 def index_rows():
@@ -87,9 +87,9 @@
     rel_ref, table_ref, const_ref, tok_ref, gmix_ref, wqkv_ref, wproj_ref, gains_ref, wup_ref, wdown_ref, pq_ref, pp_ref, pd_ref, load_sem,
     x_ref, qkv_ref, km_ref, vm_ref, s_ref, p_ref, att_ref, u1_ref, i1_ref, mid_ref, gp_ref, hid_ref, u2_ref, i2_ref,
     gup_ref, ds_ref, idx_ref, low_ref, tabf_ref, tab_ref, bias_ref, btail_ref, pk_ref, gall_ref, gsend_ref, grecv_ref, acc_ref,
-    l_ref, r_ref, o1_ref, o3_ref,
+    l_ref, r_ref, o1_ref, o2_ref, o3_ref,
     hs_ref, hr_ref,
-    sb_ref, rc_ref, wa_ref, rx_ref, wc_ref, rz_ref, wd_ref, wl_ref,
+    second_refs, early_refs, late_refs,
     tb_ref, tr1_ref, t1_ref, tr2_ref, t2_ref, t3_ref, t4_ref,
     ssem, rsem,
 ):
@@ -276,7 +276,7 @@
         u2_ref[b], i2_ref[b] = unit, inverse
         return (middle.astype(F32) + unit * gains_ref[b, 1:2, :]).astype(BF)
 
-    def backward(b, grad, between=lambda: None):
+    def backward(b, grad, after_up=lambda grad_down: None, after_scores=lambda: None):
         grad = grad.astype(F32)
         grad_down = norm_back(grad * gains_ref[b, 1:2, :], u2_ref[b], i2_ref[b]).astype(BF)
         for part in range(3):
@@ -284,7 +284,7 @@
             grad_hidden = dot(grad_down, wdown_ref[b, :, cols])
             gup_ref[b, :, cols] = (grad_hidden * gp_ref[b, :, cols]).astype(BF)
         grad_middle = grad + dot_nt(gup_ref[b], wup_ref[b])
-        between()
+        after_up(grad_down)
         grad_pre = norm_back(grad_middle * gains_ref[b, 0:1, :], u1_ref[b], i1_ref[b]).astype(BF)
         grad_att = dot_nt(grad_pre, wproj_ref[b]).astype(BF)
         q = qkv_ref[b, :, 0:C]
@@ -297,6 +297,7 @@
             ds_ref[span, :] = grad_scores.astype(BF)
             gall_ref[b, pl.ds(h, TOK, stride=8), :] = grad_scores[:, 0:128]
             gall_ref[b, pl.ds(8 * TAIL + h, 24, stride=8), :] = pack_tail(grad_scores[:, 128:TOK], h)
+        after_scores()
         grad_q = dot_tn(ds_ref[...], km_ref[b])
         grad_k, grad_v = jnp.zeros((TOK, C), F32), jnp.zeros((TOK, C), F32)
         for h in range(HEADS):
@@ -307,79 +308,111 @@
         grad_in = (grad_middle + dot_nt(grad_qkv, wqkv_ref[b])).astype(BF)
         return grad_in, grad_down, grad_pre, grad_qkv
 
-    def weight_grads(b, grad_down, grad_pre, grad_qkv):
+    def pack(buffer, piece, first_row, units):
+        z_of = piece // 4
+        for tile in range(len(units) // 2):
+            pair = jnp.concatenate([units[2 * tile], units[2 * tile + 1]], axis=0).astype(BF)
+            row = first_row + 16 * tile
+            buffer[piece % 2, z_of // 2, z_of % 2 * 2 + piece // 2 % 2, row : row + 16, :] = pair
+
+    def early_grads(b, grad_down, buffer):
+        o2_ref[...] = dot_tn(gup_ref[b], mid_ref[b, :, 0:128])
+        o3_ref[...] = dot_tn(moved(grad_down, pd_ref[...]), hid_ref[b])
+        for piece in range(32):
+            units = [o2_ref[24 * piece + 8 * i : 24 * piece + 8 * i + 8, :] for i in range(3)]
+            units += [o3_ref[8 * piece : 8 * piece + 8, 128 * i : 128 * i + 128] for i in range(6)]
+            pack(buffer, piece, 0, units + [jnp.zeros((8, 128), F32)])
+
+    def late_grads(b, grad_pre, grad_qkv, buffer, first_row):
         l_ref[0:TOK, :] = moved(grad_qkv, pq_ref[...])
         l_ref[TOK : 2 * TOK, :] = moved(grad_pre, pp_ref[...])
         l_ref[2 * TOK : 3 * TOK, :] = gup_ref[b]
-        tokens, middle = x_ref[b], mid_ref[b]
-        r_ref[0:TOK, 0:128] = tokens[:, 0:128]
-        r_ref[0:TOK, 256:320] = tokens[:, 128:C]
-        r_ref[TOK : 2 * TOK, 0:128] = att_ref[b, :, 0:128]
-        r_ref[TOK : 2 * TOK, 256:320] = att_ref[b, :, 128:C]
-        r_ref[2 * TOK : 3 * TOK, 128:256] = middle[:, 0:128]
-        r_ref[2 * TOK : 3 * TOK, 320:384] = middle[:, 128:C]
+        r_ref[0:TOK, 0:192] = x_ref[b]
+        r_ref[TOK : 2 * TOK, 0:192] = att_ref[b]
+        r_ref[2 * TOK : 3 * TOK, 192:256] = mid_ref[b, :, 128:C]
         o1_ref[...] = dot_tn(l_ref[...], r_ref[...])
-        o3_ref[...] = dot_tn(moved(grad_down, pd_ref[...]), hid_ref[b])
-        rows = 128 // n_lat
         for piece in range(32):
-            units = [o1_ref[24 * piece + 8 * i : 24 * piece + 8 * i + 8, 128 * m : 128 * m + 128] for m in range(3) for i in range(3)]
-            units += [o3_ref[8 * piece : 8 * piece + 8, 128 * i : 128 * i + 128] for i in range(6)]
-            units += [jnp.zeros((8, 128), F32)]
-            for tile in range(8):
-                pair = jnp.concatenate([units[2 * tile], units[2 * tile + 1]], axis=0).astype(BF)
-                at, off = 16 * tile // rows, 16 * tile % rows
-                across = at % 2 * 2 + piece // 2 % 2
-                sb_ref[b, piece % 2, at // 2, across, piece // 4, off : off + 16, :] = pair
+            units = [o1_ref[24 * piece + 8 * i : 24 * piece + 8 * i + 8, 128 * m : 128 * m + 128] for m in range(2) for i in range(3)]
+            pack(buffer, piece, first_row, units)
 
     class Sum:
-        def __init__(self, b):
-            self.b = b
+        def __init__(self, refs, out):
+            self.sb, self.rc, self.wa, self.rx, self.wc, self.rz, self.wl = refs
+            self.out = out
             self.copies = []
             self.steps = [self.core, self.along_xy, self.along_z, self.share, self.done]
+            self.z_sems = [next(sems) for _ in range(nz - 1)]
+            self.lat_sems = [next(sems) for _ in range(n_lat - 1)]
 
         def next(self):
             if self.steps:
                 self.steps.pop(0)()
 
         def core(self):
-            self.copies = [push(sb_ref.at[self.b, 1 - co], rc_ref.at[self.b], (lat, lon + 1 - 2 * co))]
+            self.copies = [push(self.sb.at[1 - co], self.rc, (lat, lon + 1 - 2 * co))]
 
         def along_xy(self):
-            b = self.b
             arrive(self.copies)
-            wa_ref[b] = (sb_ref[b, co].astype(F32) + rc_ref[b].astype(F32)).astype(BF)
+            self.wa[...] = (self.sb[co].astype(F32) + self.rc[...].astype(F32)).astype(BF)
             self.copies = []
             for k in range(1, 4 * ny):
                 its_y, its_x = (y + k // 4) % ny, (x + k % 4) % 4
                 device = (its_y * 2 + its_x // 2, z * 4 + its_x % 2 * 2 + co)
-                self.copies.append(push(wa_ref.at[b, its_y, its_x], rx_ref.at[b, k - 1], device))
+                self.copies.append(push(self.wa.at[its_y, its_x], self.rx.at[k - 1], device))
+
+        def to_owner(self):
+            slot = (z + nz - lat) % nz - 1
+            return pltpu.make_async_remote_copy(
+                src_ref=self.wc, dst_ref=self.rz.at[slot], send_sem=ssem.at[self.z_sems[0]],
+                recv_sem=rsem.at[self.z_sems[0] + slot], device_id=(lat, lat * 4 + xl * 2 + co), device_id_type=MESH,
+            )
+
+        def from_z(self, k):
+            return pltpu.make_async_remote_copy(
+                src_ref=self.wc, dst_ref=self.rz.at[k - 1], send_sem=ssem.at[self.z_sems[0]],
+                recv_sem=rsem.at[self.z_sems[k - 1]], device_id=(lat, z_lons[k]), device_id_type=MESH,
+            )
+
+        def to_lat(self, k):
+            return pltpu.make_async_remote_copy(
+                src_ref=self.wl, dst_ref=self.wl, send_sem=ssem.at[self.lat_sems[k - 1]],
+                recv_sem=rsem.at[self.lat_sems[0]], device_id=((lat + k) % n_lat, lon), device_id_type=MESH,
+            )
 
         def along_z(self):
-            b = self.b
             arrive(self.copies)
-            total = wa_ref[b, y, x].astype(F32)
+            total = self.wa[y, x].astype(F32)
             for k in range(4 * ny - 1):
-                total = total + rx_ref[b, k].astype(F32)
-            wc_ref[b] = total.astype(BF)
-            self.copies = []
-            for k in range(1, nz):
-                self.copies.append(push(wc_ref.at[b, (z + k) % nz], rz_ref.at[b, k - 1], (lat, z_lons[k])))
+                total = total + self.rx[k].astype(F32)
+            self.wc[...] = total.astype(BF)
+
+            @pl.when(z != lat)
+            def _():
+                self.to_owner().start()
 
         def share(self):
-            b = self.b
-            arrive(self.copies)
-            total = wc_ref[b, z].astype(F32)
-            for k in range(nz - 1):
-                total = total + rz_ref[b, k].astype(F32)
-            wd_ref[b] = total.astype(BF)
-            self.copies = []
-            for k in range(1, n_lat):
-                self.copies.append(push(wd_ref.at[b], wl_ref.at[b, lat], ((lat + k) % n_lat, lon)))
-            wl_ref[b, lat] = wd_ref[b]
+            @pl.when(z == lat)
+            def _():
+                total = self.wc[...].astype(F32)
+                for k in range(1, nz):
+                    self.from_z(k).wait_recv()
+                    total = total + self.rz[k - 1].astype(F32)
+                self.wl[...] = total.astype(BF)
+                for k in range(1, n_lat):
+                    self.to_lat(k).start()
 
         def done(self):
-            arrive(self.copies)
-            wg_ref[self.b] = wl_ref[self.b]
+            @pl.when(z != lat)
+            def _():
+                self.to_lat(1).wait_recv()
+                self.to_owner().wait_send()
+
+            self.out[...] = self.wl[...]
+
+            @pl.when(z == lat)
+            def _():
+                for k in range(1, n_lat):
+                    self.to_lat(k).wait_send()
 
     class TableSum:
         def __init__(self):
@@ -487,37 +520,52 @@
     copies_s = send_quarters(3, back)
     copies_m = send_quarters(2, back)
     copies_two = share_scores(1)
-    weight_grads(1, *rest)
-    sum_two = Sum(1)
+    grad_down, grad_pre, grad_qkv = rest
+    early_grads(1, grad_down, second_refs[0])
+    late_grads(1, grad_pre, grad_qkv, second_refs[0], 80)
+    sum_two = Sum(second_refs, wg_ref.at[1])
+    sum_early = Sum(early_refs, wg_ref.at[0, 0:80])
+    sum_late = Sum(late_refs, wg_ref.at[0, 80:128])
     sum_two.next()
 
     arrive(copies_s)
     grad_first = moved(onehot(TOK, 192, 5), hr_ref[3].reshape(192, C))
-    grad_in, *rest = backward(0, grad_first, sum_two.next)
-    copies_one = share_scores(0)
-    weight_grads(0, *rest)
-    sum_one = Sum(0)
-    sum_table = TableSum()
-    sum_one.next()
-    sum_two.next()
+    def after_up(grad_down):
+        sum_two.next()
+        early_grads(0, grad_down, early_refs[0])
+        sum_early.next()
+
+    copies_one = []
+
+    def after_scores():
+        copies_one.extend(share_scores(0))
+        sum_early.next()
+
+    grad_in, _, grad_pre, grad_qkv = backward(0, grad_first, after_up, after_scores)
     add_scores(1, copies_two)
     add_scores(0, copies_one)
-    fold_tables(0, 2)
-    sum_one.next()
-    fold_tables(2, 4)
+    fold_tables(0, 4)
+    sum_table = TableSum()
     sum_table.next()
+    late_grads(0, grad_pre, grad_qkv, late_refs[0], 0)
+    sum_late.next()
     sum_two.next()
+    sum_table.next()
+    sum_late.next()
     arrive(copies_m)
     mixed_ref[...] = moved(onehot(TOK, 192, 6), hr_ref[2].reshape(192, C)).reshape(72, 2, C)
     gtok_ref[...] = moved(onehot(TOK, TOK, 1), grad_in).reshape(72, 2, C)
+    sum_early.next()
     sum_table.next()
     sum_two.next()
+    sum_late.next()
     sum_table.next()
-    sum_one.next()
+    sum_early.next()
+    sum_late.next()
     sum_table.next()
-    sum_one.next()
-    sum_table.next()
-    sum_one.next()
+    sum_two.next()
+    sum_early.next()
+    sum_late.next()
     for copy in sent:
         copy.wait_send()
 
@@ -526,15 +574,15 @@
     mixed_ref[...] = mixed_in[...]
     gtok_ref[...] = gtok_in[...]
     for b in range(2):
-        rows = wg_in[b].reshape(128, 128).astype(F32)
-        qkv_ref[:, b, 0:128] = rows[0:18, :]
-        qkv_ref[:, b, 128:C] = rows[48:66, 0:64]
-        proj_ref[:, b, 0:128] = rows[18:24, :]
-        proj_ref[:, b, 128:C] = rows[66:72, 0:64]
-        up_ref[b, :, 0:128] = rows[24:48, :]
-        up_ref[b, :, 128:C] = rows[48:72, 64:128]
+        rows = wg_in[b].astype(F32)
+        up_ref[b, :, 0:128] = rows[0:24, :]
+        up_ref[b, :, 128:C] = rows[104:128, 64:128]
+        qkv_ref[:, b, 0:128] = rows[80:98, :]
+        qkv_ref[:, b, 128:C] = rows[104:122, 0:64]
+        proj_ref[:, b, 0:128] = rows[98:104, :]
+        proj_ref[:, b, 128:C] = rows[122:128, 0:64]
         for i in range(6):
-            down_ref[:, b, 128 * i : 128 * i + 128] = rows[72 + 8 * i : 78 + 8 * i, :]
+            down_ref[:, b, 128 * i : 128 * i + 128] = rows[24 + 8 * i : 30 + 8 * i, :]
     for part in range(26):
         tile = table_in[part // 16, part // 8 % 2, part % 8].astype(F32)
         width = min(128, POS - 128 * part)
@@ -544,12 +592,18 @@
 
 def per_device(tokens, grad_mixed, w_qkv, w_proj, w_up, w_down, gains, bias_table, rel_index, mask_ids):
     n_lat, n_lon = lax.axis_size("lat"), lax.axis_size("lon")
-    ny, nz, rows = n_lat // 2, n_lon // 4, 128 // n_lat
+    ny, nz = n_lat // 2, n_lon // 4
     vmem = pl.BlockSpec(memory_space=pltpu.VMEM)
     smem = pl.BlockSpec(memory_space=pltpu.SMEM)
 
     def buf(*shape, dtype=BF):
         return pltpu.VMEM(shape, dtype)
+
+    def stream(rows):
+        return (
+            buf(2, ny, 4, rows, 128), buf(ny, 4, rows, 128), buf(ny, 4, rows, 128), buf(4 * ny - 1, rows, 128),
+            buf(rows, 128), buf(nz - 1, rows, 128), buf(rows, 128),
+        )
 
     scratch = [
         buf(TOK, TOK, dtype=jnp.int32), buf(12, 1, POS, dtype=F32), buf(16, 768, dtype=jnp.int32),
@@ -563,11 +617,9 @@
         buf(ROWS, 128, dtype=jnp.int32), buf(ROWS // 8, 128, 8, dtype=F32), buf(2, 104, 256, dtype=F32), buf(2, 208, 256),
         buf(8 * 168, 128, dtype=F32), buf(6, 192, 128, dtype=F32), buf(6, 192, 128, dtype=F32),
         buf(2, 8 * ROWS, 128, dtype=F32), buf(2, 4 * ROWS, 128), buf(2, 4 * ROWS, 128), buf(208, 256, dtype=F32),
-        buf(3 * TOK, 768), buf(3 * TOK, 384), buf(768, 384, dtype=F32), buf(256, 768, dtype=F32),
+        buf(3 * TOK, 768), buf(3 * TOK, 256), buf(768, 256, dtype=F32), buf(768, 128, dtype=F32), buf(256, 768, dtype=F32),
         buf(4, 4, 48, C), buf(4, 4, 48, C),
-        buf(2, 2, ny, 4, nz, rows, 128), buf(2, ny, 4, nz, rows, 128), buf(2, ny, 4, nz, rows, 128),
-        buf(2, 4 * ny - 1, nz, rows, 128),
-        buf(2, nz, rows, 128), buf(2, nz - 1, rows, 128), buf(2, rows, 128), buf(2, n_lat, rows, 128),
+        stream(128), stream(80), stream(48),
         buf(2, 2, 8, 16, 128), buf(3, 8, 16, 128), buf(8, 16, 128), buf(7, 16, 128), buf(16, 128),
         buf(8, 16, 128), buf(2, 2, 8, 16, 128),
         pltpu.SemaphoreType.DMA((N_SEMS,)), pltpu.SemaphoreType.DMA((N_SEMS,)),
@@ -577,7 +629,7 @@
         out_shape=(
             jax.ShapeDtypeStruct((72, 2, C), BF),
             jax.ShapeDtypeStruct((72, 2, C), BF),
-            jax.ShapeDtypeStruct((2, n_lat, rows, 128), BF),
+            jax.ShapeDtypeStruct((2, 128, 128), BF),
             jax.ShapeDtypeStruct((2, 2, 8, 16, 128), BF),
         ),
         in_specs=[pl.BlockSpec(memory_space=pltpu.HBM)] * 13 + [smem],

time: 67.4 us -> 61.2 us (0.908)
  Pallas kernels: 66.7 us -> 59.9 us
    pallas_call x1, Pallas kernels: 64.8 us -> 58 us  [per_device(): pl.pallas_call(functools.partial(kernel, n_lat, n_lon), out_shape=(jax.Sh...]
where the time goes in v4:
time: 61.2 us; the launch traced here: 60.5 us
  Pallas kernels  59.9 us (98%)
  between operations  0.64 us (1%)
    pallas_call x1, Pallas kernels, per_device(): pl.pallas_call(functools.partial(kernel, n_lat, n_lon), out_shape=(jax.Sh...  58 us
    pallas_call x1, Pallas kernels, per_device(): pl.pallas_call(finish, out_shape=(jax.ShapeDtypeStruct((72, 2, C), BF), j...  1.89 us

profile of v4, /device:TPU:8, one launch (start us, length us, event | category | flops | bytes accessed | tf_op | source)
XLA Modules:
  0.0 60.5 jit_solution(560921534682707129)
XLA Ops:
  0.6 58.0 %shard_map.189 = (bf16[72,2,192]{2,1,0:T(2,128)(2,1)}, bf16[72,2,192]{2,1,0:T(2,128)(2,1)}, bf16[2,128,128]{2,1,0:T(8,128)(2,1)}, bf16[2,2,8,16,128]{4,3,2,1,0:T(8,128)(2,1)}) custom-call(s32[144,144]{1,0:T(8,128)} %rel_hbm.1, f32[12,1,3312]{2,1,0:T(1,128)} %bitcast.22, s32[16,768]{1,0:T(8,128)} %constant.8.clone.const_hbm, bf16[72,2,192]{2,1,0:T(2,128)(2,1)} %bitcast.23, ...), custom_call_target="tpu_custom_call" | custom-call | tf_op jit(solution)/shard_map/pallas_call | solution.py:627
  58.7 1.9 %shard_map.190 = (bf16[72,2,192]{2,1,0:T(2,128)(2,1)}, bf16[72,2,192]{2,1,0:T(2,128)(2,1)}, f32[18,2,192]{2,1,0:T(2,128)}, f32[6,2,192]{2,1,0:T(2,128)}, f32[2,2...) custom-call(bf16[72,2,192]{2,1,0:T(2,128)(2,1)} %get-tuple-element.18.mixed_in, ...), custom_call_target="tpu_custom_call" | custom-call | tf_op jit(solution)/shard_map/pallas_call | solution.py:651

commit v5 on v4

--- a/solution.py
+++ b/solution.py
@@ -68,6 +68,16 @@
     return lax.dot_general(a, b, (((0,), (0,)), ((), ())), preferred_element_type=F32)
 
 
+def normal(u):
+    power = jnp.exp(u * u * -0.5)
+    place = 1.0 / (1.0 + jnp.abs(u) * (0.3275911 * 0.5**0.5))
+    upper = 0.5 * 1.061405429
+    for term in (-1.453152027, 1.421413741, -0.284496736, 0.254829592):
+        upper = upper * place + 0.5 * term
+    upper = upper * place * power
+    return jnp.where(u < 0.0, upper, 1.0 - upper), power * 0.3989422804014327
+
+
 def norm_parts(v):
     center = v - jnp.mean(v, axis=-1, keepdims=True)
     spread = jnp.mean(center * center, axis=-1, keepdims=True)
@@ -86,7 +96,7 @@
     mixed_ref, gtok_ref, wg_ref, tgrad_ref,
     rel_ref, table_ref, const_ref, tok_ref, gmix_ref, wqkv_ref, wproj_ref, gains_ref, wup_ref, wdown_ref, pq_ref, pp_ref, pd_ref, load_sem,
     x_ref, qkv_ref, km_ref, vm_ref, s_ref, p_ref, att_ref, u1_ref, i1_ref, mid_ref, gp_ref, hid_ref, u2_ref, i2_ref,
-    gup_ref, ds_ref, idx_ref, low_ref, tabf_ref, tab_ref, bias_ref, btail_ref, pk_ref, gall_ref, gsend_ref, grecv_ref, acc_ref,
+    gup_ref, ds_ref, idx_ref, low_ref, tabf_ref, tab_ref, bias_ref, btail_ref, pk_ref, gall_ref, gsend_ref, grecv_ref, gx_ref, acc_ref,
     l_ref, r_ref, o1_ref, o2_ref, o3_ref,
     hs_ref, hr_ref,
     second_refs, early_refs, late_refs,
@@ -105,21 +115,22 @@
         load.start()
     ny, nz = n_lat // 2, n_lon // 4
     lat, lon = lax.axis_index("lat"), lax.axis_index("lon")
-    y, xh = lat // 2, lat % 2
-    z, xl, co = lon // 4, lon // 2 % 2, lon % 2
+    y, xh = lat >> 1, lat & 1
+    z, xl, co = lon >> 2, (lon >> 1) & 1, lon & 1
     x = xh * 2 + xl
-    lon_pair = [
-        (z * 4 + ((xl + (k >> 1)) % 2) * 2 + (co + (k & 1)) % 2, (xl + (k >> 1)) % 2, (co + (k & 1)) % 2)
-        for k in range(4)
-    ]
-    ahead = [((lat + n_lat - a) % n_lat, (lon + n_lon - b) % n_lon) for a in (0, 1) for b in (0, 1)]
-    back = [((lat + a) % n_lat, (lon + b) % n_lon) for a in (0, 1) for b in (0, 1)]
-    z_lons = [(z + k) % nz * 4 + xl * 2 + co for k in range(nz)]
-
-    greeted = [((lat + k) % n_lat, lon) for k in range(1, n_lat)]
+    lon_pair = [(lon ^ k, xl ^ (k >> 1), co ^ (k & 1)) for k in range(4)]
+    lats = [(lat + k) & (n_lat - 1) for k in range(n_lat)]
+    ahead = [((lat - a) & (n_lat - 1), (lon - b) & (n_lon - 1)) for a in (0, 1) for b in (0, 1)]
+    back = [((lat + a) & (n_lat - 1), (lon + b) & (n_lon - 1)) for a in (0, 1) for b in (0, 1)]
+    z_lons = [(lon + 4 * k) & (n_lon - 1) for k in range(nz)]
+    ys, xs = [(y + k) & (ny - 1) for k in range(ny)], [(x + k) & 3 for k in range(4)]
+    xy_lons = [lon - xl * 2 + (its_x & 1) * 2 for its_x in xs]
+    xy_lats = [[its_y * 2 + (its_x >> 1) for its_x in xs] for its_y in ys]
+
+    greeted = [(lats[k], lon) for k in range(1, n_lat)]
     greeted += [(lat, z_lons[k]) for k in range(1, nz)]
     greeted += [(lat, lon_pair[k][0]) for k in (1, 3)]
-    greeted += [((lat + k) % n_lat, lon_pair[2][0]) for k in range(n_lat)]
+    greeted += [(lats[k], lon_pair[2][0]) for k in range(n_lat)]
     greeted += [ahead[1], ahead[3], back[1], back[3]]
     barrier = pltpu.get_barrier_semaphore()
     for device in greeted:
@@ -171,8 +182,8 @@
         one, zero = jnp.ones((256, 128), BF), jnp.zeros((256, 128), BF)
 
         def step(i, carry):
-            for m in range(3):
-                group = i * 3 + m
+            for m in range(7):
+                group = i * 7 + m
                 index = idx_ref[pl.ds(pl.multiple_of(group * 8, 8), 8), :]
                 low, high = (index & 255).astype(F32), index >> 8
                 picks = []
@@ -190,7 +201,7 @@
                     bias_ref[pl.ds(pl.multiple_of(group * 64 + r * 8, 8), 8), :] = found
             return carry
 
-        lax.fori_loop(0, 7, step, 0)
+        lax.fori_loop(0, 3, step, 0)
         for h in range(HEADS):
             unpack_tail(bias_ref[pl.ds(8 * TAIL + h, 24, stride=8), :], h)
 
@@ -198,39 +209,42 @@
 
     def share_scores(b):
         gsend_ref[b] = gall_ref[b, pl.ds((1 - co) * 8 * half, 8 * half), :].astype(BF)
-        return [push(gsend_ref.at[b], grecv_ref.at[b], (lat, lon + 1 - 2 * co))]
-
-    def add_scores(b, copies):
-        arrive(copies)
-        mine = pl.ds(co * 8 * half, 8 * half)
-        gall_ref[b, mine, :] = gall_ref[b, mine, :] + grecv_ref[b].astype(F32)
-
-    def fold_tables(start, stop):
+        return [push(gsend_ref.at[b], grecv_ref.at[b], (lat, lon_pair[1][0]))]
+
+    def add_scores(copies):
+        both = []
+        for b in range(2):
+            arrive(copies[b])
+            total = gall_ref[b, pl.ds(co * 8 * half, 8 * half), :] + grecv_ref[b].astype(F32)
+            both.append(total.reshape(half, 8, 128))
+        gx_ref[...] = jnp.concatenate(both, axis=1).astype(BF)
+
+    def fold_tables():
         place = lax.broadcasted_iota(jnp.int32, (128, 256), 1).astype(BF)
         one, zero = jnp.ones((128, 256), BF), jnp.zeros((128, 256), BF)
+        nothing = jnp.zeros((16, 128), BF)
 
         def step(i, carry):
             total = acc_ref[...]
-            for m in range(3):
-                group = co * (half // 8) + i * 3 + m
-                high = idx_ref[pl.ds(pl.multiple_of(group * 8, 8), 8), :] >> 8
+            for m in range(6):
+                group = i * 6 + m
+                start = pl.multiple_of(co * half + group * 8, 8)
+                high = (idx_ref[pl.ds(start, 8), :] >> 8).astype(F32)
                 block = low_ref[group]
-                left, right = [[] for _ in range(26)], []
+                left, right = [[] for _ in range(13)], []
                 for r in range(8):
-                    high_row = jnp.broadcast_to(high[r : r + 1, :], (8, 128))
-                    hits = [high_row == part for part in range(13)]
-                    for b in range(2):
-                        grads = gall_ref[b, pl.ds(pl.multiple_of(group * 64 + r * 8, 8), 8), :]
-                        for part in range(13):
-                            left[13 * b + part].append(jnp.where(hits[part], grads, 0.0))
+                    high_row = jnp.broadcast_to(high[r : r + 1, :], (16, 128)).astype(BF)
+                    grads = gx_ref[group * 8 + r]
+                    for part in range(13):
+                        left[part].append(jnp.where(high_row == jnp.full((16, 128), part, BF), grads, nothing))
                     column = jnp.broadcast_to(block[:, r : r + 1], (128, 128)).astype(BF)
                     right.append(jnp.where(place == jnp.concatenate([column] * 2, axis=1), one, zero))
-                left = jnp.concatenate([jnp.concatenate(rows, axis=1) for rows in left], axis=0).astype(BF)
+                left = jnp.concatenate([jnp.concatenate(rows, axis=1) for rows in left], axis=0)
                 total = total + dot(left, jnp.concatenate(right, axis=0))
             acc_ref[...] = total
             return carry
 
-        lax.fori_loop(start, stop, step, 0)
+        lax.fori_loop(0, 2, step, 0)
 
     def region_codes(place):
         code = jnp.zeros_like(place)
@@ -269,9 +283,9 @@
         for part in range(3):
             cols = pl.ds(256 * part, 256)
             up = dot(middle, wup_ref[b, :, cols])
-            phi = 0.5 + 0.5 * lax.erf(up * (0.5**0.5))
+            phi, density = normal(up)
             hid_ref[b, :, cols] = (up * phi).astype(BF)
-            gp_ref[b, :, cols] = phi + up * (0.3989422804014327 * jnp.exp(-0.5 * up * up))
+            gp_ref[b, :, cols] = phi + up * density
         unit, inverse = norm_parts(dot_nt(hid_ref[b], wdown_ref[b]))
         u2_ref[b], i2_ref[b] = unit, inverse
         return (middle.astype(F32) + unit * gains_ref[b, 1:2, :]).astype(BF)
@@ -349,19 +363,18 @@
                 self.steps.pop(0)()
 
         def core(self):
-            self.copies = [push(self.sb.at[1 - co], self.rc, (lat, lon + 1 - 2 * co))]
+            self.copies = [push(self.sb.at[1 - co], self.rc, (lat, lon_pair[1][0]))]
 
         def along_xy(self):
             arrive(self.copies)
             self.wa[...] = (self.sb[co].astype(F32) + self.rc[...].astype(F32)).astype(BF)
             self.copies = []
             for k in range(1, 4 * ny):
-                its_y, its_x = (y + k // 4) % ny, (x + k % 4) % 4
-                device = (its_y * 2 + its_x // 2, z * 4 + its_x % 2 * 2 + co)
-                self.copies.append(push(self.wa.at[its_y, its_x], self.rx.at[k - 1], device))
+                device = (xy_lats[k // 4][k % 4], xy_lons[k % 4])
+                self.copies.append(push(self.wa.at[ys[k // 4], xs[k % 4]], self.rx.at[k - 1], device))
 
         def to_owner(self):
-            slot = (z + nz - lat) % nz - 1
+            slot = ((z - lat) & (nz - 1)) - 1
             return pltpu.make_async_remote_copy(
                 src_ref=self.wc, dst_ref=self.rz.at[slot], send_sem=ssem.at[self.z_sems[0]],
                 recv_sem=rsem.at[self.z_sems[0] + slot], device_id=(lat, lat * 4 + xl * 2 + co), device_id_type=MESH,
@@ -376,7 +389,7 @@
         def to_lat(self, k):
             return pltpu.make_async_remote_copy(
                 src_ref=self.wl, dst_ref=self.wl, send_sem=ssem.at[self.lat_sems[k - 1]],
-                recv_sem=rsem.at[self.lat_sems[0]], device_id=((lat + k) % n_lat, lon), device_id_type=MESH,
+                recv_sem=rsem.at[self.lat_sems[0]], device_id=(lats[k], lon), device_id_type=MESH,
             )
 
         def along_z(self):
@@ -425,8 +438,8 @@
 
         def pair(self):
             for part in range(26):
-                row, lanes = 8 * (part // 2), slice(128 * (part % 2), 128 * (part % 2) + 128)
-                both = jnp.concatenate([acc_ref[row : row + 8, lanes], acc_ref[104 + row : 112 + row, lanes]], axis=0)
+                row, lanes = 16 * (part // 2), slice(128 * (part % 2), 128 * (part % 2) + 128)
+                both = acc_ref[row : row + 16, lanes]
                 tb_ref[part // 16, part // 8 % 2, part % 8] = both.astype(BF)
             for part in range(26, 32):
                 tb_ref[part // 16, part // 8 % 2, part % 8] = jnp.zeros((16, 128), BF)
@@ -442,7 +455,7 @@
             t1_ref[...] = total.astype(BF)
             self.copies = []
             for k in range(1, nz):
-                self.copies.append(push(t1_ref.at[(z + k) % nz], tr2_ref.at[k - 1], (lat, z_lons[k])))
+                self.copies.append(push(t1_ref.at[(z + k) & (nz - 1)], tr2_ref.at[k - 1], (lat, z_lons[k])))
 
         def share_z(self):
             arrive(self.copies)
@@ -481,8 +494,8 @@
     idx_ref[0:TOK, :] = relative[:, 0:128].astype(jnp.int32)
     idx_ref[TAIL : TAIL + 24, :] = pack_tail(relative[:, 128:TOK], 0).astype(jnp.int32)
     idx_ref[TAIL + 18 : ROWS, :] = jnp.full((ROWS - TAIL - 18, 128), -1, jnp.int32)
-    low = (idx_ref[...] & 255).astype(F32).T
-    for i in range(ROWS // 8):
+    low = (idx_ref[pl.ds(pl.multiple_of(co * half, 8), half), :] & 255).astype(F32).T
+    for i in range(half // 8):
         low_ref[i] = low[:, 8 * i : 8 * i + 8]
     loads[1].wait()
     tabf_ref[...] = jnp.zeros_like(tabf_ref)
@@ -542,9 +555,8 @@
         sum_early.next()
 
     grad_in, _, grad_pre, grad_qkv = backward(0, grad_first, after_up, after_scores)
-    add_scores(1, copies_two)
-    add_scores(0, copies_one)
-    fold_tables(0, 4)
+    add_scores([copies_one, copies_two])
+    fold_tables()
     sum_table = TableSum()
     sum_table.next()
     late_grads(0, grad_pre, grad_qkv, late_refs[0], 0)
@@ -614,9 +626,10 @@
         buf(2, 6 * TOK, TOK), buf(2, TOK, C), buf(2, TOK, C, dtype=F32), buf(2, TOK, 1, dtype=F32), buf(2, TOK, C),
         buf(2, TOK, 768, dtype=F32), buf(2, TOK, 768), buf(2, TOK, C, dtype=F32), buf(2, TOK, 1, dtype=F32),
         buf(2, TOK, 768), buf(6 * TOK, TOK),
-        buf(ROWS, 128, dtype=jnp.int32), buf(ROWS // 8, 128, 8, dtype=F32), buf(2, 104, 256, dtype=F32), buf(2, 208, 256),
+        buf(ROWS, 128, dtype=jnp.int32), buf(ROWS // 16, 128, 8, dtype=F32), buf(2, 104, 256, dtype=F32), buf(2, 208, 256),
         buf(8 * 168, 128, dtype=F32), buf(6, 192, 128, dtype=F32), buf(6, 192, 128, dtype=F32),
-        buf(2, 8 * ROWS, 128, dtype=F32), buf(2, 4 * ROWS, 128), buf(2, 4 * ROWS, 128), buf(208, 256, dtype=F32),
+        buf(2, 8 * ROWS, 128, dtype=F32), buf(2, 4 * ROWS, 128), buf(2, 4 * ROWS, 128),
+        buf(ROWS // 2, 16, 128), buf(208, 256, dtype=F32),
         buf(3 * TOK, 768), buf(3 * TOK, 256), buf(768, 256, dtype=F32), buf(768, 128, dtype=F32), buf(256, 768, dtype=F32),
         buf(4, 4, 48, C), buf(4, 4, 48, C),
         stream(128), stream(80), stream(48),

time: 61.2 us -> 60.6 us (level)
    pallas_call x1, Pallas kernels: 58 us -> 57.4 us  [per_device(): pl.pallas_call(functools.partial(kernel, n_lat, n_lon), out_shape=(jax.Sh...]
where the time goes in v5:
time: 60.6 us; the launch traced here: 59.9 us
  Pallas kernels  59.3 us (98%)
  between operations  0.64 us (1%)
    pallas_call x1, Pallas kernels, per_device(): pl.pallas_call(functools.partial(kernel, n_lat, n_lon), out_shape=(jax.Sh...  57.4 us
    pallas_call x1, Pallas kernels, per_device(): pl.pallas_call(finish, out_shape=(jax.ShapeDtypeStruct((72, 2, C), BF), j...  1.89 us

profile of v5, /device:TPU:8, one launch (start us, length us, event | category | flops | bytes accessed | tf_op | source)
XLA Modules:
  0.0 59.9 jit_solution(12383552788573390911)
XLA Ops:
  0.6 57.4 %shard_map.189 = (bf16[72,2,192]{2,1,0:T(2,128)(2,1)}, bf16[72,2,192]{2,1,0:T(2,128)(2,1)}, bf16[2,128,128]{2,1,0:T(8,128)(2,1)}, bf16[2,2,8,16,128]{4,3,2,1,0:T(8,128)(2,1)}) custom-call(s32[144,144]{1,0:T(8,128)} %rel_hbm.1, f32[12,1,3312]{2,1,0:T(1,128)} %bitcast.22, s32[16,768]{1,0:T(8,128)} %constant.8.clone.const_hbm, bf16[72,2,192]{2,1,0:T(2,128)(2,1)} %bitcast.23, ...), custom_call_target="tpu_custom_call" | custom-call | tf_op jit(solution)/shard_map/pallas_call | solution.py:640
  58.0 1.9 %shard_map.190 = (bf16[72,2,192]{2,1,0:T(2,128)(2,1)}, bf16[72,2,192]{2,1,0:T(2,128)(2,1)}, f32[18,2,192]{2,1,0:T(2,128)}, f32[6,2,192]{2,1,0:T(2,128)}, f32[2,2...) custom-call(bf16[72,2,192]{2,1,0:T(2,128)(2,1)} %get-tuple-element.18.mixed_in, ...), custom_call_target="tpu_custom_call" | custom-call | tf_op jit(solution)/shard_map/pallas_call | solution.py:664

commit v6 on v5

--- a/solution.py
+++ b/solution.py
@@ -53,7 +53,7 @@
         for i in range(6):
             proj[6 * piece + i, 24 * piece + 18 + i] = 1
             down[6 * piece + i, 8 * piece + i] = 1
-    return tuple(jnp.asarray(matrix, BF) for matrix in (qkv, proj, down))
+    return tuple(jnp.asarray(matrix, BF) for matrix in (qkv.T, proj.T, down.T, np.eye(256, dtype=np.float32)))
 
 
 def dot(a, b):
@@ -92,12 +92,12 @@
 
 def kernel(
     n_lat, n_lon,
-    rel_hbm, table_hbm, const_hbm, tok_hbm, gmix_hbm, wqkv_hbm, wproj_hbm, gains_hbm, wup_hbm, wdown_hbm, pq_hbm, pp_hbm, pd_hbm, ids_ref,
+    rel_hbm, table_hbm, const_hbm, tok_hbm, gmix_hbm, wqkv_hbm, wproj_hbm, gains_hbm, wup_hbm, wdown_hbm, pq_hbm, pp_hbm, pd_hbm, eye_hbm, ids_ref,
     mixed_ref, gtok_ref, wg_ref, tgrad_ref,
-    rel_ref, table_ref, const_ref, tok_ref, gmix_ref, wqkv_ref, wproj_ref, gains_ref, wup_ref, wdown_ref, pq_ref, pp_ref, pd_ref, load_sem,
+    rel_ref, table_ref, const_ref, tok_ref, gmix_ref, wqkv_ref, wproj_ref, gains_ref, wup_ref, wdown_ref, pq_ref, pp_ref, pd_ref, eye_ref, load_sem,
     x_ref, qkv_ref, km_ref, vm_ref, s_ref, p_ref, att_ref, u1_ref, i1_ref, mid_ref, gp_ref, hid_ref, u2_ref, i2_ref,
     gup_ref, ds_ref, idx_ref, low_ref, tabf_ref, tab_ref, bias_ref, btail_ref, pk_ref, gall_ref, gsend_ref, grecv_ref, gx_ref, acc_ref,
-    l_ref, r_ref, o1_ref, o2_ref, o3_ref,
+    r_ref, o1_ref, o2_ref, o3_ref,
     hs_ref, hr_ref,
     second_refs, early_refs, late_refs,
     tb_ref, tr1_ref, t1_ref, tr2_ref, t2_ref, t3_ref, t4_ref,
@@ -108,7 +108,7 @@
         for k, (src, dst) in enumerate([
             (rel_hbm, rel_ref), (table_hbm, table_ref), (const_hbm, const_ref), (tok_hbm, tok_ref), (gmix_hbm, gmix_ref),
             (wqkv_hbm, wqkv_ref), (wproj_hbm, wproj_ref), (gains_hbm, gains_ref), (wup_hbm, wup_ref), (wdown_hbm, wdown_ref),
-            (pq_hbm, pq_ref), (pp_hbm, pp_ref), (pd_hbm, pd_ref),
+            (pq_hbm, pq_ref), (pp_hbm, pp_ref), (pd_hbm, pd_ref), (eye_hbm, eye_ref),
         ])
     ]
     for load in loads:
@@ -128,7 +128,7 @@
     xy_lats = [[its_y * 2 + (its_x >> 1) for its_x in xs] for its_y in ys]
 
     greeted = [(lats[k], lon) for k in range(1, n_lat)]
-    greeted += [(lat, z_lons[k]) for k in range(1, nz)]
+    greeted += [(lat, z_lons[k] ^ flip) for k in range(1, nz) for flip in (0, 2)]
     greeted += [(lat, lon_pair[k][0]) for k in (1, 3)]
     greeted += [(lats[k], lon_pair[2][0]) for k in range(n_lat)]
     greeted += [ahead[1], ahead[3], back[1], back[3]]
@@ -322,32 +322,41 @@
         grad_in = (grad_middle + dot_nt(grad_qkv, wqkv_ref[b])).astype(BF)
         return grad_in, grad_down, grad_pre, grad_qkv
 
-    def pack(buffer, piece, first_row, units):
-        z_of = piece // 4
+    def by_owner(buffer, piece):
+        return buffer.at[piece % 2, piece // 8, piece // 4 % 2 * 2 + piece // 2 % 2]
+
+    def by_lon(buffer, piece):
+        return buffer.at[piece % 2, piece // 4, piece // 2 % 2]
+
+    def pack(place, first_row, units):
         for tile in range(len(units) // 2):
             pair = jnp.concatenate([units[2 * tile], units[2 * tile + 1]], axis=0).astype(BF)
             row = first_row + 16 * tile
-            buffer[piece % 2, z_of // 2, z_of % 2 * 2 + piece // 2 % 2, row : row + 16, :] = pair
+            place[row : row + 16, :] = pair
 
     def early_grads(b, grad_down, buffer):
-        o2_ref[...] = dot_tn(gup_ref[b], mid_ref[b, :, 0:128])
-        o3_ref[...] = dot_tn(moved(grad_down, pd_ref[...]), hid_ref[b])
+        r_ref[:, 0:128] = mid_ref[b, :, 0:128]
+        r_ref[:, C:256] = mid_ref[b, :, 128:C]
+        for part in range(3):
+            span = slice(256 * part, 256 * part + 256)
+            turned = dot_nt(eye_ref[...], gup_ref[b, :, span]).astype(BF)
+            grads = dot(turned, r_ref[...])
+            o2_ref[span, :] = grads[:, 0:128]
+            o1_ref[span, C:256] = grads[:, C:256]
+        o3_ref[...] = dot(dot_nt(pd_ref[...], grad_down).astype(BF), hid_ref[b])
         for piece in range(32):
             units = [o2_ref[24 * piece + 8 * i : 24 * piece + 8 * i + 8, :] for i in range(3)]
             units += [o3_ref[8 * piece : 8 * piece + 8, 128 * i : 128 * i + 128] for i in range(6)]
-            pack(buffer, piece, 0, units + [jnp.zeros((8, 128), F32)])
-
-    def late_grads(b, grad_pre, grad_qkv, buffer, first_row):
-        l_ref[0:TOK, :] = moved(grad_qkv, pq_ref[...])
-        l_ref[TOK : 2 * TOK, :] = moved(grad_pre, pp_ref[...])
-        l_ref[2 * TOK : 3 * TOK, :] = gup_ref[b]
-        r_ref[0:TOK, 0:192] = x_ref[b]
-        r_ref[TOK : 2 * TOK, 0:192] = att_ref[b]
-        r_ref[2 * TOK : 3 * TOK, 192:256] = mid_ref[b, :, 128:C]
-        o1_ref[...] = dot_tn(l_ref[...], r_ref[...])
+            pack(by_owner(buffer, piece), 0, units + [jnp.zeros((8, 128), F32)])
+
+    def late_grads(b, grad_pre, grad_qkv, buffer, layout, first_row):
+        turned = dot_nt(pp_ref[...], grad_pre).astype(BF)
+        grads = dot(turned, att_ref[b])
+        turned = dot_nt(pq_ref[...], grad_qkv).astype(BF)
+        o1_ref[:, 0:C] = grads + dot(turned, x_ref[b])
         for piece in range(32):
             units = [o1_ref[24 * piece + 8 * i : 24 * piece + 8 * i + 8, 128 * m : 128 * m + 128] for m in range(2) for i in range(3)]
-            pack(buffer, piece, first_row, units)
+            pack(layout(buffer, piece), first_row, units)
 
     class Sum:
         def __init__(self, refs, out):
@@ -426,6 +435,38 @@
             def _():
                 for k in range(1, n_lat):
                     self.to_lat(k).wait_send()
+
+    class LateSum(Sum):
+        def __init__(self, refs, out):
+            self.sb, self.rc, self.wa, self.rx, self.wc, self.wl = refs
+            self.out = out
+            self.copies = []
+            self.steps = [self.core, self.along_zx, self.share, self.done]
+
+        def along_zx(self):
+            arrive(self.copies)
+            self.wa[...] = (self.sb[co].astype(F32) + self.rc[...].astype(F32)).astype(BF)
+            self.copies = []
+            for k in range(1, 2 * nz):
+                device = (lat, z_lons[k >> 1] ^ (2 * (k & 1)))
+                target = self.wa.at[(z + (k >> 1)) & (nz - 1), xl ^ (k & 1)]
+                self.copies.append(push(target, self.rx.at[k - 1], device))
+
+        def share(self):
+            arrive(self.copies)
+            total = self.wa[z, xl].astype(F32)
+            for k in range(2 * nz - 1):
+                total = total + self.rx[k].astype(F32)
+            self.wc[...] = total.astype(BF)
+            self.copies = [push(self.wc, self.wl.at[lat], (lats[k], lon)) for k in range(1, n_lat)]
+            self.wl[lat] = self.wc[...]
+
+        def done(self):
+            arrive(self.copies)
+            total = self.wl[0].astype(F32)
+            for k in range(1, n_lat):
+                total = total + self.wl[k].astype(F32)
+            self.out[...] = total.astype(BF)
 
     class TableSum:
         def __init__(self):
@@ -535,10 +576,10 @@
     copies_two = share_scores(1)
     grad_down, grad_pre, grad_qkv = rest
     early_grads(1, grad_down, second_refs[0])
-    late_grads(1, grad_pre, grad_qkv, second_refs[0], 80)
+    late_grads(1, grad_pre, grad_qkv, second_refs[0], by_owner, 80)
     sum_two = Sum(second_refs, wg_ref.at[1])
     sum_early = Sum(early_refs, wg_ref.at[0, 0:80])
-    sum_late = Sum(late_refs, wg_ref.at[0, 80:128])
+    sum_late = LateSum(late_refs, wg_ref.at[0, 80:128])
     sum_two.next()
 
     arrive(copies_s)
@@ -559,7 +600,7 @@
     fold_tables()
     sum_table = TableSum()
     sum_table.next()
-    late_grads(0, grad_pre, grad_qkv, late_refs[0], 0)
+    late_grads(0, grad_pre, grad_qkv, late_refs[0], by_lon, 0)
     sum_late.next()
     sum_two.next()
     sum_table.next()
@@ -571,13 +612,12 @@
     sum_table.next()
     sum_two.next()
     sum_late.next()
-    sum_table.next()
     sum_early.next()
-    sum_late.next()
     sum_table.next()
     sum_two.next()
+    sum_late.next()
     sum_early.next()
-    sum_late.next()
+    sum_table.next()
     for copy in sent:
         copy.wait_send()
 
@@ -620,8 +660,8 @@
     scratch = [
         buf(TOK, TOK, dtype=jnp.int32), buf(12, 1, POS, dtype=F32), buf(16, 768, dtype=jnp.int32),
         buf(72, 2, C), buf(72, 2, C), buf(2, C, 3 * C), buf(2, C, C), buf(2, 2, C, dtype=F32), buf(2, C, 768), buf(2, C, 768),
-        buf(3 * C, 768), buf(C, 768), buf(C, 256),
-        pltpu.SemaphoreType.DMA((13,)),
+        buf(768, 3 * C), buf(768, C), buf(256, C), buf(256, 256),
+        pltpu.SemaphoreType.DMA((14,)),
         buf(2, TOK, C), buf(2, TOK, 3 * C), buf(2, 6 * TOK, C), buf(2, 6 * TOK, C), buf(6 * TOK, TOK, dtype=F32),
         buf(2, 6 * TOK, TOK), buf(2, TOK, C), buf(2, TOK, C, dtype=F32), buf(2, TOK, 1, dtype=F32), buf(2, TOK, C),
         buf(2, TOK, 768, dtype=F32), buf(2, TOK, 768), buf(2, TOK, C, dtype=F32), buf(2, TOK, 1, dtype=F32),
@@ -630,9 +670,13 @@
         buf(8 * 168, 128, dtype=F32), buf(6, 192, 128, dtype=F32), buf(6, 192, 128, dtype=F32),
         buf(2, 8 * ROWS, 128, dtype=F32), buf(2, 4 * ROWS, 128), buf(2, 4 * ROWS, 128),
         buf(ROWS // 2, 16, 128), buf(208, 256, dtype=F32),
-        buf(3 * TOK, 768), buf(3 * TOK, 256), buf(768, 256, dtype=F32), buf(768, 128, dtype=F32), buf(256, 768, dtype=F32),
+        buf(TOK, 256), buf(768, 256, dtype=F32), buf(768, 128, dtype=F32), buf(256, 768, dtype=F32),
         buf(4, 4, 48, C), buf(4, 4, 48, C),
-        stream(128), stream(80), stream(48),
+        stream(128), stream(80),
+        (
+            buf(2, nz, 2, 48, 128), buf(nz, 2, 48, 128), buf(nz, 2, 48, 128), buf(2 * nz - 1, 48, 128),
+            buf(48, 128), buf(n_lat, 48, 128),
+        ),
         buf(2, 2, 8, 16, 128), buf(3, 8, 16, 128), buf(8, 16, 128), buf(7, 16, 128), buf(16, 128),
         buf(8, 16, 128), buf(2, 2, 8, 16, 128),
         pltpu.SemaphoreType.DMA((N_SEMS,)), pltpu.SemaphoreType.DMA((N_SEMS,)),
@@ -645,7 +689,7 @@
             jax.ShapeDtypeStruct((2, 128, 128), BF),
             jax.ShapeDtypeStruct((2, 2, 8, 16, 128), BF),
         ),
-        in_specs=[pl.BlockSpec(memory_space=pltpu.HBM)] * 13 + [smem],
+        in_specs=[pl.BlockSpec(memory_space=pltpu.HBM)] * 14 + [smem],
         out_specs=[vmem] * 4,
         scratch_shapes=scratch,
         compiler_params=pltpu.CompilerParams(

time: 60.6 us -> 63.1 us (1.041)
  the two profiles are of different devices: /device:TPU:8 before, /device:TPU:1 now
where the time goes in v6:
time: 63.1 us; the launch traced here: 63 us
  Pallas kernels  62.4 us (99%)
  between operations  0.64 us (1%)
    pallas_call x1, Pallas kernels, per_device(): pl.pallas_call(functools.partial(kernel, n_lat, n_lon), out_shape=(jax.Sh...  60.5 us
    pallas_call x1, Pallas kernels, per_device(): pl.pallas_call(finish, out_shape=(jax.ShapeDtypeStruct((72, 2, C), BF), j...  1.89 us

profile of v6, /device:TPU:1, one launch (start us, length us, event | category | flops | bytes accessed | tf_op | source)
XLA Modules:
  0.0 63.0 jit_solution(11354509846003474290)
XLA Ops:
  0.6 60.5 %shard_map.198 = (bf16[72,2,192]{2,1,0:T(2,128)(2,1)}, bf16[72,2,192]{2,1,0:T(2,128)(2,1)}, bf16[2,128,128]{2,1,0:T(8,128)(2,1)}, bf16[2,2,8,16,128]{4,3,2,1,0:T(8,128)(2,1)}) custom-call(s32[144,144]{1,0:T(8,128)} %rel_hbm.1, f32[12,1,3312]{2,1,0:T(1,128)} %bitcast.22, s32[16,768]{1,0:T(8,128)} %constant.10.clone.const_hbm, bf16[72,2,192]{2,1,0:T(2,128)(2,1)} %bitcast.23, ...), custom_call_target="tpu_custom_call" | custom-call | tf_op jit(solution)/shard_map/pallas_call | solution.py:684
  61.1 1.9 %shard_map.199 = (bf16[72,2,192]{2,1,0:T(2,128)(2,1)}, bf16[72,2,192]{2,1,0:T(2,128)(2,1)}, f32[18,2,192]{2,1,0:T(2,128)}, f32[6,2,192]{2,1,0:T(2,128)}, f32[2,2...) custom-call(bf16[72,2,192]{2,1,0:T(2,128)(2,1)} %get-tuple-element.18.mixed_in, ...), custom_call_target="tpu_custom_call" | custom-call | tf_op jit(solution)/shard_map/pallas_call | solution.py:708

commit v7 on v6

--- a/solution.py
+++ b/solution.py
@@ -93,7 +93,7 @@
 def kernel(
     n_lat, n_lon,
     rel_hbm, table_hbm, const_hbm, tok_hbm, gmix_hbm, wqkv_hbm, wproj_hbm, gains_hbm, wup_hbm, wdown_hbm, pq_hbm, pp_hbm, pd_hbm, eye_hbm, ids_ref,
-    mixed_ref, gtok_ref, wg_ref, tgrad_ref,
+    mixed_ref, gtok_ref, gqkv_out, gproj_out, gup_out, gdown_out, tgrad_ref,
     rel_ref, table_ref, const_ref, tok_ref, gmix_ref, wqkv_ref, wproj_ref, gains_ref, wup_ref, wdown_ref, pq_ref, pp_ref, pd_ref, eye_ref, load_sem,
     x_ref, qkv_ref, km_ref, vm_ref, s_ref, p_ref, att_ref, u1_ref, i1_ref, mid_ref, gp_ref, hid_ref, u2_ref, i2_ref,
     gup_ref, ds_ref, idx_ref, low_ref, tabf_ref, tab_ref, bias_ref, btail_ref, pk_ref, gall_ref, gsend_ref, grecv_ref, gx_ref, acc_ref,
@@ -128,7 +128,7 @@
     xy_lats = [[its_y * 2 + (its_x >> 1) for its_x in xs] for its_y in ys]
 
     greeted = [(lats[k], lon) for k in range(1, n_lat)]
-    greeted += [(lat, z_lons[k] ^ flip) for k in range(1, nz) for flip in (0, 2)]
+    greeted += [(lat, z_lons[k]) for k in range(1, nz)]
     greeted += [(lat, lon_pair[k][0]) for k in (1, 3)]
     greeted += [(lats[k], lon_pair[2][0]) for k in range(n_lat)]
     greeted += [ahead[1], ahead[3], back[1], back[3]]
@@ -319,14 +319,14 @@
             grad_k = jnp.where(head_lanes[h], dot(ds_ref[span, :], q), grad_k)
             grad_v = jnp.where(head_lanes[h], dot(p_ref[b, span, :], grad_att), grad_v)
         grad_qkv = jnp.concatenate([grad_q * SCALE, grad_k * SCALE, grad_v], axis=1).astype(BF)
-        grad_in = (grad_middle + dot_nt(grad_qkv, wqkv_ref[b])).astype(BF)
+
+        def grad_in():
+            return (grad_middle + dot_nt(grad_qkv, wqkv_ref[b])).astype(BF)
+
         return grad_in, grad_down, grad_pre, grad_qkv
 
     def by_owner(buffer, piece):
         return buffer.at[piece % 2, piece // 8, piece // 4 % 2 * 2 + piece // 2 % 2]
-
-    def by_lon(buffer, piece):
-        return buffer.at[piece % 2, piece // 4, piece // 2 % 2]
 
     def pack(place, first_row, units):
         for tile in range(len(units) // 2):
@@ -349,19 +349,18 @@
             units += [o3_ref[8 * piece : 8 * piece + 8, 128 * i : 128 * i + 128] for i in range(6)]
             pack(by_owner(buffer, piece), 0, units + [jnp.zeros((8, 128), F32)])
 
-    def late_grads(b, grad_pre, grad_qkv, buffer, layout, first_row):
+    def late_grads(b, grad_pre, grad_qkv, buffer, first_row):
         turned = dot_nt(pp_ref[...], grad_pre).astype(BF)
         grads = dot(turned, att_ref[b])
         turned = dot_nt(pq_ref[...], grad_qkv).astype(BF)
         o1_ref[:, 0:C] = grads + dot(turned, x_ref[b])
         for piece in range(32):
             units = [o1_ref[24 * piece + 8 * i : 24 * piece + 8 * i + 8, 128 * m : 128 * m + 128] for m in range(2) for i in range(3)]
-            pack(layout(buffer, piece), first_row, units)
+            pack(by_owner(buffer, piece), first_row, units)
 
     class Sum:
-        def __init__(self, refs, out):
+        def __init__(self, refs):
             self.sb, self.rc, self.wa, self.rx, self.wc, self.rz, self.wl = refs
-            self.out = out
             self.copies = []
             self.steps = [self.core, self.along_xy, self.along_z, self.share, self.done]
             self.z_sems = [next(sems) for _ in range(nz - 1)]
@@ -429,44 +428,10 @@
                 self.to_lat(1).wait_recv()
                 self.to_owner().wait_send()
 
-            self.out[...] = self.wl[...]
-
             @pl.when(z == lat)
             def _():
                 for k in range(1, n_lat):
                     self.to_lat(k).wait_send()
-
-    class LateSum(Sum):
-        def __init__(self, refs, out):
-            self.sb, self.rc, self.wa, self.rx, self.wc, self.wl = refs
-            self.out = out
-            self.copies = []
-            self.steps = [self.core, self.along_zx, self.share, self.done]
-
-        def along_zx(self):
-            arrive(self.copies)
-            self.wa[...] = (self.sb[co].astype(F32) + self.rc[...].astype(F32)).astype(BF)
-            self.copies = []
-            for k in range(1, 2 * nz):
-                device = (lat, z_lons[k >> 1] ^ (2 * (k & 1)))
-                target = self.wa.at[(z + (k >> 1)) & (nz - 1), xl ^ (k & 1)]
-                self.copies.append(push(target, self.rx.at[k - 1], device))
-
-        def share(self):
-            arrive(self.copies)
-            total = self.wa[z, xl].astype(F32)
-            for k in range(2 * nz - 1):
-                total = total + self.rx[k].astype(F32)
-            self.wc[...] = total.astype(BF)
-            self.copies = [push(self.wc, self.wl.at[lat], (lats[k], lon)) for k in range(1, n_lat)]
-            self.wl[lat] = self.wc[...]
-
-        def done(self):
-            arrive(self.copies)
-            total = self.wl[0].astype(F32)
-            for k in range(1, n_lat):
-                total = total + self.wl[k].astype(F32)
-            self.out[...] = total.astype(BF)
 
     class TableSum:
         def __init__(self):
@@ -518,7 +483,15 @@
 
         def done(self):
             arrive(self.copies)
-            tgrad_ref[...] = t4_ref[...]
+
+    def write_grads(b, rows):
+        gup_out[b, :, 0:128] = rows[0:24, :]
+        for i in range(6):
+            gdown_out[:, b, 128 * i : 128 * i + 128] = rows[24 + 8 * i : 30 + 8 * i, :]
+        main, tail = rows[80:104, :], rows[104:128, :]
+        gqkv_out[:, b, 0:128], gproj_out[:, b, 0:128] = main[0:18, :], main[18:24, :]
+        gqkv_out[:, b, 128:C], gproj_out[:, b, 128:C] = tail[0:18, 0:64], tail[18:24, 0:64]
+        gup_out[b, :, 128:C] = tail[:, 64:128]
 
     def send_quarters(which, devices):
         copies = []
@@ -570,16 +543,14 @@
     second = forward(1)
     hs_ref[2] = moved(onehot(192, TOK, 4), second).reshape(4, 48, C)
     grad_second, *rest = backward(1, grad_shifted)
-    hs_ref[3] = moved(onehot(192, TOK, 4), grad_second).reshape(4, 48, C)
+    hs_ref[3] = moved(onehot(192, TOK, 4), grad_second()).reshape(4, 48, C)
     copies_s = send_quarters(3, back)
     copies_m = send_quarters(2, back)
     copies_two = share_scores(1)
     grad_down, grad_pre, grad_qkv = rest
     early_grads(1, grad_down, second_refs[0])
-    late_grads(1, grad_pre, grad_qkv, second_refs[0], by_owner, 80)
-    sum_two = Sum(second_refs, wg_ref.at[1])
-    sum_early = Sum(early_refs, wg_ref.at[0, 0:80])
-    sum_late = LateSum(late_refs, wg_ref.at[0, 80:128])
+    late_grads(1, grad_pre, grad_qkv, second_refs[0], 80)
+    sum_two, sum_early, sum_late = Sum(second_refs), Sum(early_refs), Sum(late_refs)
     sum_two.next()
 
     arrive(copies_s)
@@ -600,46 +571,43 @@
     fold_tables()
     sum_table = TableSum()
     sum_table.next()
-    late_grads(0, grad_pre, grad_qkv, late_refs[0], by_lon, 0)
+    sum_two.next()
+    late_grads(0, grad_pre, grad_qkv, late_refs[0], 0)
     sum_late.next()
-    sum_two.next()
     sum_table.next()
     sum_late.next()
+    gtok_ref[...] = moved(onehot(TOK, TOK, 1), grad_in()).reshape(72, 2, C)
+    sum_table.next()
+    sum_early.next()
     arrive(copies_m)
     mixed_ref[...] = moved(onehot(TOK, 192, 6), hr_ref[2].reshape(192, C)).reshape(72, 2, C)
-    gtok_ref[...] = moved(onehot(TOK, TOK, 1), grad_in).reshape(72, 2, C)
-    sum_early.next()
     sum_table.next()
     sum_two.next()
     sum_late.next()
     sum_early.next()
+    sum_late.next()
+    sum_two.next()
+    write_grads(1, second_refs[-1][...].astype(F32))
     sum_table.next()
-    sum_two.next()
+    for part in range(26):
+        tile = t4_ref[part // 16, part // 8 % 2, part % 8].astype(F32)
+        width = min(128, POS - 128 * part)
+        for b in range(2):
+            tgrad_ref[6 * b : 6 * b + 6, 0, 128 * part : 128 * part + width] = tile[8 * b : 8 * b + 6, 0:width]
+    sum_early.next()
     sum_late.next()
-    sum_early.next()
-    sum_table.next()
+    write_grads(0, jnp.concatenate([early_refs[-1][...].astype(F32), late_refs[-1][...].astype(F32)], axis=0))
     for copy in sent:
         copy.wait_send()
 
 
-def finish(mixed_in, gtok_in, wg_in, table_in, mixed_ref, gtok_ref, qkv_ref, proj_ref, up_ref, down_ref, table_ref):
-    mixed_ref[...] = mixed_in[...]
-    gtok_ref[...] = gtok_in[...]
-    for b in range(2):
-        rows = wg_in[b].astype(F32)
-        up_ref[b, :, 0:128] = rows[0:24, :]
-        up_ref[b, :, 128:C] = rows[104:128, 64:128]
-        qkv_ref[:, b, 0:128] = rows[80:98, :]
-        qkv_ref[:, b, 128:C] = rows[104:122, 0:64]
-        proj_ref[:, b, 0:128] = rows[98:104, :]
-        proj_ref[:, b, 128:C] = rows[122:128, 0:64]
-        for i in range(6):
-            down_ref[:, b, 128 * i : 128 * i + 128] = rows[24 + 8 * i : 30 + 8 * i, :]
-    for part in range(26):
-        tile = table_in[part // 16, part // 8 % 2, part % 8].astype(F32)
-        width = min(128, POS - 128 * part)
-        for b in range(2):
-            table_ref[6 * b : 6 * b + 6, 0, 128 * part : 128 * part + width] = tile[8 * b : 8 * b + 6, 0:width]
+def hand_over(*refs):
+    sources, targets, sems = refs[:7], refs[7:14], refs[14]
+    copies = [pltpu.make_async_copy(source, target, sems.at[k]) for k, (source, target) in enumerate(zip(sources, targets))]
+    for copy in copies:
+        copy.start()
+    for copy in copies:
+        copy.wait()
 
 
 def per_device(tokens, grad_mixed, w_qkv, w_proj, w_up, w_down, gains, bias_table, rel_index, mask_ids):
@@ -672,25 +640,25 @@
         buf(ROWS // 2, 16, 128), buf(208, 256, dtype=F32),
         buf(TOK, 256), buf(768, 256, dtype=F32), buf(768, 128, dtype=F32), buf(256, 768, dtype=F32),
         buf(4, 4, 48, C), buf(4, 4, 48, C),
-        stream(128), stream(80),
-        (
-            buf(2, nz, 2, 48, 128), buf(nz, 2, 48, 128), buf(nz, 2, 48, 128), buf(2 * nz - 1, 48, 128),
-            buf(48, 128), buf(n_lat, 48, 128),
-        ),
+        stream(128), stream(80), stream(48),
         buf(2, 2, 8, 16, 128), buf(3, 8, 16, 128), buf(8, 16, 128), buf(7, 16, 128), buf(16, 128),
         buf(8, 16, 128), buf(2, 2, 8, 16, 128),
         pltpu.SemaphoreType.DMA((N_SEMS,)), pltpu.SemaphoreType.DMA((N_SEMS,)),
     ]
+    shapes = (
+        jax.ShapeDtypeStruct((72, 2, C), BF),
+        jax.ShapeDtypeStruct((72, 2, C), BF),
+        jax.ShapeDtypeStruct((18, 2, C), F32),
+        jax.ShapeDtypeStruct((6, 2, C), F32),
+        jax.ShapeDtypeStruct((2, 24, C), F32),
+        jax.ShapeDtypeStruct((6, 2, 768), F32),
+        jax.ShapeDtypeStruct((12, 1, POS), F32),
+    )
     results = pl.pallas_call(
         functools.partial(kernel, n_lat, n_lon),
-        out_shape=(
-            jax.ShapeDtypeStruct((72, 2, C), BF),
-            jax.ShapeDtypeStruct((72, 2, C), BF),
-            jax.ShapeDtypeStruct((2, 128, 128), BF),
-            jax.ShapeDtypeStruct((2, 2, 8, 16, 128), BF),
-        ),
+        out_shape=shapes,
         in_specs=[pl.BlockSpec(memory_space=pltpu.HBM)] * 14 + [smem],
-        out_specs=[vmem] * 4,
+        out_specs=[vmem] * 7,
         scratch_shapes=scratch,
         compiler_params=pltpu.CompilerParams(
             collective_id=0, has_side_effects=True, vmem_limit_bytes=60 * 1024 * 1024
@@ -706,18 +674,11 @@
         mask_ids,
     )
     mixed, grad_tokens, qkv, proj, up, down, table = pl.pallas_call(
-        finish,
-        out_shape=(
-            jax.ShapeDtypeStruct((72, 2, C), BF),
-            jax.ShapeDtypeStruct((72, 2, C), BF),
-            jax.ShapeDtypeStruct((18, 2, C), F32),
-            jax.ShapeDtypeStruct((6, 2, C), F32),
-            jax.ShapeDtypeStruct((2, 24, C), F32),
-            jax.ShapeDtypeStruct((6, 2, 768), F32),
-            jax.ShapeDtypeStruct((12, 1, POS), F32),
-        ),
-        in_specs=[vmem] * 4,
-        out_specs=[vmem] * 7,
+        hand_over,
+        out_shape=shapes,
+        in_specs=[pl.BlockSpec(memory_space=pltpu.HBM)] * 7,
+        out_specs=[pl.BlockSpec(memory_space=pltpu.HBM)] * 7,
+        scratch_shapes=[pltpu.SemaphoreType.DMA((7,))],
         compiler_params=pltpu.CompilerParams(vmem_limit_bytes=60 * 1024 * 1024),
     )(*results)
 

time: 63.1 us -> 76.7 us (1.22)
  the two profiles are of different devices: /device:TPU:1 before, /device:TPU:8 now
where the time goes in v7:
time: 76.7 us; the launch traced here: 75.6 us
  Pallas kernels  74.8 us (98%)
  between operations  0.8 us (1%)
    pallas_call x1, Pallas kernels, per_device(): pl.pallas_call(functools.partial(kernel, n_lat, n_lon), out_shape=shapes,...  60.3 us
    pallas_call x1, Pallas kernels, per_device(): pl.pallas_call(hand_over, out_shape=shapes, in_specs=[pl.BlockSpec(memory...  14.6 us

profile of v7, /device:TPU:8, one launch (start us, length us, event | category | flops | bytes accessed | tf_op | source)
XLA Modules:
  0.0 75.6 jit_solution(5628112330498945282)
XLA Ops:
  0.6 60.3 %shard_map.198 = (bf16[72,2,192]{2,1,0:T(2,128)(2,1)}, bf16[72,2,192]{2,1,0:T(2,128)(2,1)}, f32[18,2,192]{2,1,0:T(2,128)}, f32[6,2,192]{2,1,0:T(2,128)}, f32[2,2...) custom-call(s32[144,144]{1,0:T(8,128)} %rel_hbm.1, f32[12,1,3312]{2,1,0:T(1,128)} %bitcast.22, ...), custom_call_target="tpu_custom_call" | custom-call | tf_op jit(solution)/shard_map/pallas_call | solution.py:657
  60.9 14.6 %shard_map.199 = (bf16[72,2,192]{2,1,0:T(2,128)(2,1)}, bf16[72,2,192]{2,1,0:T(2,128)(2,1)}, f32[18,2,192]{2,1,0:T(2,128)}, f32[6,2,192]{2,1,0:T(2,128)}, f32[2,2...) custom-call(bf16[72,2,192]{2,1,0:T(2,128)(2,1)} %get-tuple-element.21.refs_0_, ...), custom_call_target="tpu_custom_call" | custom-call | tf_op jit(solution)/shard_map/pallas_call | solution.py:676

commit v8 on v7

--- a/solution.py
+++ b/solution.py
@@ -93,10 +93,10 @@
 def kernel(
     n_lat, n_lon,
     rel_hbm, table_hbm, const_hbm, tok_hbm, gmix_hbm, wqkv_hbm, wproj_hbm, gains_hbm, wup_hbm, wdown_hbm, pq_hbm, pp_hbm, pd_hbm, eye_hbm, ids_ref,
-    mixed_ref, gtok_ref, gqkv_out, gproj_out, gup_out, gdown_out, tgrad_ref,
+    mixed_ref, gtok_ref, wg_ref, tgrad_ref,
     rel_ref, table_ref, const_ref, tok_ref, gmix_ref, wqkv_ref, wproj_ref, gains_ref, wup_ref, wdown_ref, pq_ref, pp_ref, pd_ref, eye_ref, load_sem,
     x_ref, qkv_ref, km_ref, vm_ref, s_ref, p_ref, att_ref, u1_ref, i1_ref, mid_ref, gp_ref, hid_ref, u2_ref, i2_ref,
-    gup_ref, ds_ref, idx_ref, low_ref, tabf_ref, tab_ref, bias_ref, btail_ref, pk_ref, gall_ref, gsend_ref, grecv_ref, gx_ref, acc_ref,
+    gup_ref, ds_ref, idx_ref, low_ref, tabf_ref, tab_ref, bias_ref, btail_ref, pk_ref, gall_ref, gsend_ref, grecv_ref, gx_ref, oht_ref, acc_ref,
     r_ref, o1_ref, o2_ref, o3_ref,
     hs_ref, hr_ref,
     second_refs, early_refs, late_refs,
@@ -211,37 +211,37 @@
         gsend_ref[b] = gall_ref[b, pl.ds((1 - co) * 8 * half, 8 * half), :].astype(BF)
         return [push(gsend_ref.at[b], grecv_ref.at[b], (lat, lon_pair[1][0]))]
 
-    def add_scores(copies):
-        both = []
-        for b in range(2):
-            arrive(copies[b])
-            total = gall_ref[b, pl.ds(co * 8 * half, 8 * half), :] + grecv_ref[b].astype(F32)
-            both.append(total.reshape(half, 8, 128))
-        gx_ref[...] = jnp.concatenate(both, axis=1).astype(BF)
-
-    def fold_tables():
+    def fold_table(b, copies):
+        arrive(copies)
+        gx_ref[...] = gall_ref[b, pl.ds(co * 8 * half, 8 * half), :] + grecv_ref[b].astype(F32)
         place = lax.broadcasted_iota(jnp.int32, (128, 256), 1).astype(BF)
         one, zero = jnp.ones((128, 256), BF), jnp.zeros((128, 256), BF)
-        nothing = jnp.zeros((16, 128), BF)
 
         def step(i, carry):
-            total = acc_ref[...]
+            total = acc_ref[b]
             for m in range(6):
                 group = i * 6 + m
                 start = pl.multiple_of(co * half + group * 8, 8)
-                high = (idx_ref[pl.ds(start, 8), :] >> 8).astype(F32)
-                block = low_ref[group]
-                left, right = [[] for _ in range(13)], []
+                high = idx_ref[pl.ds(start, 8), :] >> 8
+                left = [[] for _ in range(13)]
                 for r in range(8):
-                    high_row = jnp.broadcast_to(high[r : r + 1, :], (16, 128)).astype(BF)
-                    grads = gx_ref[group * 8 + r]
+                    high_row = jnp.broadcast_to(high[r : r + 1, :], (8, 128))
+                    grads = gx_ref[pl.ds(pl.multiple_of(group * 64 + r * 8, 8), 8), :]
                     for part in range(13):
-                        left[part].append(jnp.where(high_row == jnp.full((16, 128), part, BF), grads, nothing))
-                    column = jnp.broadcast_to(block[:, r : r + 1], (128, 128)).astype(BF)
-                    right.append(jnp.where(place == jnp.concatenate([column] * 2, axis=1), one, zero))
-                left = jnp.concatenate([jnp.concatenate(rows, axis=1) for rows in left], axis=0)
-                total = total + dot(left, jnp.concatenate(right, axis=0))
-            acc_ref[...] = total
+                        left[part].append(jnp.where(high_row == part, grads, 0.0))
+                left = jnp.concatenate([jnp.concatenate(rows, axis=1) for rows in left], axis=0).astype(BF)
+                span = pl.ds(pl.multiple_of(group * 1024, 1024), 1024)
+                if b == 1:
+                    block, right = low_ref[group], []
+                    for r in range(8):
+                        column = jnp.broadcast_to(block[:, r : r + 1], (128, 128)).astype(BF)
+                        right.append(jnp.where(place == jnp.concatenate([column] * 2, axis=1), one, zero))
+                    right = jnp.concatenate(right, axis=0)
+                    oht_ref[span, :] = right
+                else:
+                    right = oht_ref[span, :]
+                total = total + dot(left, right)
+            acc_ref[b] = total
             return carry
 
         lax.fori_loop(0, 2, step, 0)
@@ -444,8 +444,8 @@
 
         def pair(self):
             for part in range(26):
-                row, lanes = 16 * (part // 2), slice(128 * (part % 2), 128 * (part % 2) + 128)
-                both = acc_ref[row : row + 16, lanes]
+                row, lanes = 8 * (part // 2), slice(128 * (part % 2), 128 * (part % 2) + 128)
+                both = jnp.concatenate([acc_ref[b, row : row + 8, lanes] for b in range(2)], axis=0)
                 tb_ref[part // 16, part // 8 % 2, part % 8] = both.astype(BF)
             for part in range(26, 32):
                 tb_ref[part // 16, part // 8 % 2, part % 8] = jnp.zeros((16, 128), BF)
@@ -483,15 +483,6 @@
 
         def done(self):
             arrive(self.copies)
-
-    def write_grads(b, rows):
-        gup_out[b, :, 0:128] = rows[0:24, :]
-        for i in range(6):
-            gdown_out[:, b, 128 * i : 128 * i + 128] = rows[24 + 8 * i : 30 + 8 * i, :]
-        main, tail = rows[80:104, :], rows[104:128, :]
-        gqkv_out[:, b, 0:128], gproj_out[:, b, 0:128] = main[0:18, :], main[18:24, :]
-        gqkv_out[:, b, 128:C], gproj_out[:, b, 128:C] = tail[0:18, 0:64], tail[18:24, 0:64]
-        gup_out[b, :, 128:C] = tail[:, 64:128]
 
     def send_quarters(which, devices):
         copies = []
@@ -555,59 +546,66 @@
 
     arrive(copies_s)
     grad_first = moved(onehot(TOK, 192, 5), hr_ref[3].reshape(192, C))
+    sum_two.next()
+    sum_table = TableSum()
+
     def after_up(grad_down):
-        sum_two.next()
         early_grads(0, grad_down, early_refs[0])
         sum_early.next()
 
-    copies_one = []
-
     def after_scores():
-        copies_one.extend(share_scores(0))
+        copies_one = share_scores(0)
         sum_early.next()
+        fold_table(1, copies_two)
+        fold_table(0, copies_one)
+        sum_table.next()
 
     grad_in, _, grad_pre, grad_qkv = backward(0, grad_first, after_up, after_scores)
-    add_scores([copies_one, copies_two])
-    fold_tables()
-    sum_table = TableSum()
-    sum_table.next()
-    sum_two.next()
     late_grads(0, grad_pre, grad_qkv, late_refs[0], 0)
     sum_late.next()
     sum_table.next()
+    sum_two.next()
     sum_late.next()
     gtok_ref[...] = moved(onehot(TOK, TOK, 1), grad_in()).reshape(72, 2, C)
-    sum_table.next()
-    sum_early.next()
     arrive(copies_m)
     mixed_ref[...] = moved(onehot(TOK, 192, 6), hr_ref[2].reshape(192, C)).reshape(72, 2, C)
     sum_table.next()
+    sum_early.next()
     sum_two.next()
+    sum_table.next()
     sum_late.next()
     sum_early.next()
     sum_late.next()
+    sum_table.next()
+    tgrad_ref[...] = t4_ref[...]
     sum_two.next()
-    write_grads(1, second_refs[-1][...].astype(F32))
-    sum_table.next()
+    wg_ref[1] = second_refs[-1][...]
+    sum_early.next()
+    wg_ref[0, 0:80, :] = early_refs[-1][...]
+    sum_late.next()
+    wg_ref[0, 80:128, :] = late_refs[-1][...]
+    for copy in sent:
+        copy.wait_send()
+
+
+def finish(mixed_in, gtok_in, wg_in, table_in, mixed_ref, gtok_ref, qkv_ref, proj_ref, up_ref, down_ref, table_ref):
+    mixed_ref[...] = mixed_in[...]
+    gtok_ref[...] = gtok_in[...]
+    for b in range(2):
+        rows = wg_in[b].astype(F32)
+        up_ref[b, :, 0:128] = rows[0:24, :]
+        up_ref[b, :, 128:C] = rows[104:128, 64:128]
+        qkv_ref[:, b, 0:128] = rows[80:98, :]
+        qkv_ref[:, b, 128:C] = rows[104:122, 0:64]
+        proj_ref[:, b, 0:128] = rows[98:104, :]
+        proj_ref[:, b, 128:C] = rows[122:128, 0:64]
+        for i in range(6):
+            down_ref[:, b, 128 * i : 128 * i + 128] = rows[24 + 8 * i : 30 + 8 * i, :]
     for part in range(26):
-        tile = t4_ref[part // 16, part // 8 % 2, part % 8].astype(F32)
+        tile = table_in[part // 16, part // 8 % 2, part % 8].astype(F32)
         width = min(128, POS - 128 * part)
         for b in range(2):
-            tgrad_ref[6 * b : 6 * b + 6, 0, 128 * part : 128 * part + width] = tile[8 * b : 8 * b + 6, 0:width]
-    sum_early.next()
-    sum_late.next()
-    write_grads(0, jnp.concatenate([early_refs[-1][...].astype(F32), late_refs[-1][...].astype(F32)], axis=0))
-    for copy in sent:
-        copy.wait_send()
-
-
-def hand_over(*refs):
-    sources, targets, sems = refs[:7], refs[7:14], refs[14]
-    copies = [pltpu.make_async_copy(source, target, sems.at[k]) for k, (source, target) in enumerate(zip(sources, targets))]
-    for copy in copies:
-        copy.start()
-    for copy in copies:
-        copy.wait()
+            table_ref[6 * b : 6 * b + 6, 0, 128 * part : 128 * part + width] = tile[8 * b : 8 * b + 6, 0:width]
 
 
 def per_device(tokens, grad_mixed, w_qkv, w_proj, w_up, w_down, gains, bias_table, rel_index, mask_ids):
@@ -637,7 +635,7 @@
         buf(ROWS, 128, dtype=jnp.int32), buf(ROWS // 16, 128, 8, dtype=F32), buf(2, 104, 256, dtype=F32), buf(2, 208, 256),
         buf(8 * 168, 128, dtype=F32), buf(6, 192, 128, dtype=F32), buf(6, 192, 128, dtype=F32),
         buf(2, 8 * ROWS, 128, dtype=F32), buf(2, 4 * ROWS, 128), buf(2, 4 * ROWS, 128),
-        buf(ROWS // 2, 16, 128), buf(208, 256, dtype=F32),
+        buf(4 * ROWS, 128, dtype=F32), buf(64 * ROWS, 256), buf(2, 104, 256, dtype=F32),
         buf(TOK, 256), buf(768, 256, dtype=F32), buf(768, 128, dtype=F32), buf(256, 768, dtype=F32),
         buf(4, 4, 48, C), buf(4, 4, 48, C),
         stream(128), stream(80), stream(48),
@@ -656,9 +654,14 @@
     )
     results = pl.pallas_call(
         functools.partial(kernel, n_lat, n_lon),
-        out_shape=shapes,
+        out_shape=(
+            jax.ShapeDtypeStruct((72, 2, C), BF),
+            jax.ShapeDtypeStruct((72, 2, C), BF),
+            jax.ShapeDtypeStruct((2, 128, 128), BF),
+            jax.ShapeDtypeStruct((2, 2, 8, 16, 128), BF),
+        ),
         in_specs=[pl.BlockSpec(memory_space=pltpu.HBM)] * 14 + [smem],
-        out_specs=[vmem] * 7,
+        out_specs=[vmem] * 4,
         scratch_shapes=scratch,
         compiler_params=pltpu.CompilerParams(
             collective_id=0, has_side_effects=True, vmem_limit_bytes=60 * 1024 * 1024
@@ -674,11 +677,10 @@
         mask_ids,
     )
     mixed, grad_tokens, qkv, proj, up, down, table = pl.pallas_call(
-        hand_over,
+        finish,
         out_shape=shapes,
-        in_specs=[pl.BlockSpec(memory_space=pltpu.HBM)] * 7,
-        out_specs=[pl.BlockSpec(memory_space=pltpu.HBM)] * 7,
-        scratch_shapes=[pltpu.SemaphoreType.DMA((7,))],
+        in_specs=[vmem] * 4,
+        out_specs=[vmem] * 7,
         compiler_params=pltpu.CompilerParams(vmem_limit_bytes=60 * 1024 * 1024),
     )(*results)
 

time: 76.7 us -> 64 us (0.83)
  Pallas kernels: 74.8 us -> 62.5 us
    pallas_call x2, Pallas kernels: 74.8 us -> 62.5 us  [the longest x1 60.6 us: per_device(): pl.pallas_call(functools.partial(kernel, n_lat, n_lon), out_shape=(jax.Sh...]
where the time goes in v8:
time: 64 us; the launch traced here: 63.1 us
  Pallas kernels  62.5 us (98%)
  between operations  0.64 us (1%)
    pallas_call x1, Pallas kernels, per_device(): pl.pallas_call(functools.partial(kernel, n_lat, n_lon), out_shape=(jax.Sh...  60.6 us
    pallas_call x1, Pallas kernels, per_device(): pl.pallas_call(finish, out_shape=shapes, in_specs=[vmem] * 4, out_specs=[...  1.89 us

profile of v8, /device:TPU:8, one launch (start us, length us, event | category | flops | bytes accessed | tf_op | source)
XLA Modules:
  0.0 63.1 jit_solution(876796713575752835)
XLA Ops:
  0.6 60.6 %shard_map.198 = (bf16[72,2,192]{2,1,0:T(2,128)(2,1)}, bf16[72,2,192]{2,1,0:T(2,128)(2,1)}, bf16[2,128,128]{2,1,0:T(8,128)(2,1)}, bf16[2,2,8,16,128]{4,3,2,1,0:T(8,128)(2,1)}) custom-call(s32[144,144]{1,0:T(8,128)} %rel_hbm.1, f32[12,1,3312]{2,1,0:T(1,128)} %bitcast.22, s32[16,768]{1,0:T(8,128)} %constant.10.clone.const_hbm, bf16[72,2,192]{2,1,0:T(2,128)(2,1)} %bitcast.23, ...), custom_call_target="tpu_custom_call" | custom-call | tf_op jit(solution)/shard_map/pallas_call | solution.py:655
  61.2 1.9 %shard_map.199 = (bf16[72,2,192]{2,1,0:T(2,128)(2,1)}, bf16[72,2,192]{2,1,0:T(2,128)(2,1)}, f32[18,2,192]{2,1,0:T(2,128)}, f32[6,2,192]{2,1,0:T(2,128)}, f32[2,2...) custom-call(bf16[72,2,192]{2,1,0:T(2,128)(2,1)} %get-tuple-element.18.mixed_in, ...), custom_call_target="tpu_custom_call" | custom-call | tf_op jit(solution)/shard_map/pallas_call | solution.py:679

commit v9 on v5

--- a/solution.py
+++ b/solution.py
@@ -543,8 +543,9 @@
 
     arrive(copies_s)
     grad_first = moved(onehot(TOK, 192, 5), hr_ref[3].reshape(192, C))
+    sum_two.next()
+
     def after_up(grad_down):
-        sum_two.next()
         early_grads(0, grad_down, early_refs[0])
         sum_early.next()
 

time: 60.6 us -> 60.1 us (level)
  no operation moved by 1% of the time
where the time goes in v9:
time: 60.1 us; the launch traced here: 59.4 us
  Pallas kernels  58.8 us (98%)
  between operations  0.64 us (1%)
    pallas_call x1, Pallas kernels, per_device(): pl.pallas_call(functools.partial(kernel, n_lat, n_lon), out_shape=(jax.Sh...  56.9 us
    pallas_call x1, Pallas kernels, per_device(): pl.pallas_call(finish, out_shape=(jax.ShapeDtypeStruct((72, 2, C), BF), j...  1.89 us

profile of v9, /device:TPU:8, one launch (start us, length us, event | category | flops | bytes accessed | tf_op | source)
XLA Modules:
  0.0 59.4 jit_solution(9234608301030096049)
XLA Ops:
  0.6 56.9 %shard_map.189 = (bf16[72,2,192]{2,1,0:T(2,128)(2,1)}, bf16[72,2,192]{2,1,0:T(2,128)(2,1)}, bf16[2,128,128]{2,1,0:T(8,128)(2,1)}, bf16[2,2,8,16,128]{4,3,2,1,0:T(8,128)(2,1)}) custom-call(s32[144,144]{1,0:T(8,128)} %rel_hbm.1, f32[12,1,3312]{2,1,0:T(1,128)} %bitcast.22, s32[16,768]{1,0:T(8,128)} %constant.8.clone.const_hbm, bf16[72,2,192]{2,1,0:T(2,128)(2,1)} %bitcast.23, ...), custom_call_target="tpu_custom_call" | custom-call | tf_op jit(solution)/shard_map/pallas_call | solution.py:641
  57.6 1.9 %shard_map.190 = (bf16[72,2,192]{2,1,0:T(2,128)(2,1)}, bf16[72,2,192]{2,1,0:T(2,128)(2,1)}, f32[18,2,192]{2,1,0:T(2,128)}, f32[6,2,192]{2,1,0:T(2,128)}, f32[2,2...) custom-call(bf16[72,2,192]{2,1,0:T(2,128)(2,1)} %get-tuple-element.18.mixed_in, ...), custom_call_target="tpu_custom_call" | custom-call | tf_op jit(solution)/shard_map/pallas_call | solution.py:665
